TPU v7x, 128 devices: a whole 4x4x4 slice. The times are simulated.
128 devices in a mesh: gx: 8 (over z, core), gy: 16 (over y, x).
Axes of the slice: x: 4, y: 4, z: 4, core: 2. Of those that a mesh axis runs over, the one named last changes fastest.
Arguments:
- dyn_state: bfloat16 [40, 64, 65536], P(None, None, ('gx', 'gy')), may hold values from -6 to 6
- span_map: int32 [65536], P(('gx', 'gy')), may hold values from 0 to 65535, as said below
- sunlit: int32 [65536], P(('gx', 'gy')), may hold values from 0 to 1, as said below
- coszen: float32 [65536], P(('gx', 'gy')), may hold values from 0.05 to 1
- albedo: float32 [65536], P(('gx', 'gy')), may hold values from 0.05 to 0.9
- ground_temp: float32 [65536], P(('gx', 'gy')), may hold values from -6 to 6
- aerosol: bfloat16 [58, 64, 65536], P(None, None, ('gx', 'gy')), may hold values from -6 to 6
- k_long: bfloat16 [128, 98], replicated, may hold values from -1 to 1
- planck: float32 [128], replicated, may hold values from 0.25 to 0.5
- k_short: bfloat16 [112, 98], replicated, may hold values from -0.625 to 0.625
- solar_flux: float32 [112], replicated, may hold values from 2 to 8
Outputs:
- heating: float32 [64, 65536], P(None, ('gx', 'gy'))
- surface: float32 [2, 65536], P(None, ('gx', 'gy'))
Inputs may be any that keep to these rules, and one draw needn't show every extreme that they name: span_map is a permutation of 0 .. 65535. Of the 512 columns of a device, exactly 64 have span positions on the same device (position // 512 equal to the device's index along gx+gy); to every other device it sends either 4 or 3 columns, and 4 to some. At most 448 of a device's 512 span-order columns are sunlit, and some device has exactly 448. Two devices at the same gy index whose gx indices differ by half of gx's size hold together at most 512 sunlit columns.
All inputs are finite; a program needn't handle non-finite values.
Results may differ from a plain program's by a relative error of at most 0.0005.
Values may be sent and summed in bfloat16 or wider, within the bound.
No kernel may reach another device: no remote copies, remote signals or barrier semaphores. Data moves between devices by JAX's collectives and lax.ppermute only.
A program may use at most 128 MiB of HBM per device.

v0:
```python
import functools

import jax
import jax.numpy as jnp
from jax import lax
from jax.experimental import pallas as pl
from jax.experimental.pallas import tpu as pltpu
from jax.sharding import PartitionSpec as P

AXES = ("gx", "gy")
DIFFUSE = 1.66
SCATTER = 0.3
SW_DEPTH = 2.0
LOG2E = 1.4426950408889634
CAP = 4
BF16 = jnp.bfloat16
F32 = jnp.float32
NT = (((1,), (1,)), ((), ()))
TN = (((0,), (0,)), ((), ()))
MIB = 1 << 20


def onehot(mask):
    return jnp.where(mask, 1.0, 0.0).astype(BF16)


def halves(x):
    high = x.astype(BF16)
    return high, (x - high.astype(F32)).astype(BF16)


def softplus2(u):
    return jnp.maximum(u, jnp.log2(1.0 + jnp.exp2(jnp.minimum(u, 126.0))))


def pack_kernel(me_ref, map_ref, dyn_ref, out_ref, pick_ref, meta_ref, rows_ref):
    devices = out_ref.shape[0] // (2 * CAP)
    columns = map_ref.shape[1]
    step = pl.program_id(0)
    last = pl.num_programs(0) - 1

    @pl.when(step == 0)
    def _():
        where_to = map_ref[...]
        target = where_to // columns
        slot = where_to % columns
        same = target == lax.broadcasted_iota(jnp.int32, (devices, columns), 0)
        earlier = onehot(
            lax.broadcasted_iota(jnp.int32, (columns, columns), 0)
            < lax.broadcasted_iota(jnp.int32, (columns, columns), 1)
        )
        before = jnp.dot(onehot(same), earlier, preferred_element_type=F32)
        rank = jnp.sum(jnp.where(same, before, 0.0), axis=0, keepdims=True).astype(jnp.int32)
        rank = jnp.where(target == me_ref[0], CAP, rank)
        for place in range(CAP):
            pick_ref[place * devices : (place + 1) * devices, :] = onehot(same & (rank == place))
        line = lax.broadcasted_iota(jnp.int32, (128, columns), 0)
        mark = slot + 1
        meta = jnp.where(line == 0, mark // 2, jnp.where(line == 1, mark % 2, 0))
        meta_ref[...] = meta.astype(F32).astype(BF16)

    def put(part, half):
        moved = lax.dot_general(pick_ref[...], part, NT, preferred_element_type=F32)
        for place in range(CAP):
            rows_ref[pl.ds(place * 2 + half, devices, stride=2 * CAP), :] = moved[
                place * devices : (place + 1) * devices
            ]

    @pl.when(step < last)
    def _():
        for half in range(2):
            put(dyn_ref[:, half * 32 : half * 32 + 32, :].reshape(128, columns), half)

    @pl.when(step == last)
    def _():
        for half in range(2):
            put(meta_ref[...], half)

    out_ref[...] = rows_ref[...].astype(BF16)


def pack(me, map_row, dyn_state, devices):
    fields, levels, columns = dyn_state.shape
    steps = fields // 4
    return pl.pallas_call(
        pack_kernel,
        grid=(steps + 1,),
        in_specs=[
            pl.BlockSpec(memory_space=pltpu.SMEM),
            pl.BlockSpec((1, columns), lambda i: (0, 0)),
            pl.BlockSpec((4, levels, columns), lambda i: (jnp.minimum(i, steps - 1), 0, 0)),
        ],
        out_specs=[
            pl.BlockSpec((devices * CAP * 2, 128), lambda i: (0, i)),
            pl.BlockSpec((devices * CAP, columns), lambda i: (0, 0)),
        ],
        out_shape=[
            jax.ShapeDtypeStruct((devices * CAP * 2, (steps + 1) * 128), BF16),
            jax.ShapeDtypeStruct((devices * CAP, columns), BF16),
        ],
        scratch_shapes=[
            pltpu.VMEM((128, columns), BF16),
            pltpu.VMEM((devices * CAP * 2, 128), F32),
        ],
        compiler_params=pltpu.CompilerParams(vmem_limit_bytes=32 * MIB),
        cost_estimate=pl.CostEstimate(
            flops=2 * fields * levels * columns * devices * CAP, bytes_accessed=6 * MIB, transcendentals=0
        ),
        name="pack",
    )(me, map_row, dyn_state)


def base_kernel(me_ref, map_ref, dyn_ref, aer_ref, out_ref, pick_ref, rows_ref):
    fields, depth, columns = dyn_ref.shape
    extra = aer_ref.shape[0]
    first = out_ref.shape[1] - 64

    @pl.when(pl.program_id(0) == 0)
    def _():
        goal = lax.broadcasted_iota(jnp.int32, (columns, columns), 0) + me_ref[0] * columns
        pick_ref[...] = onehot(map_ref[...] == goal)

    kept = lax.dot_general(
        dyn_ref[...].reshape(fields * depth, columns), pick_ref[...], NT, preferred_element_type=F32
    )
    tall = fields * depth
    more = aer_ref[...].reshape(extra * depth, columns).astype(F32)
    for tile in range(columns // 128):
        lanes = slice(tile * 128, tile * 128 + 128)
        rows_ref[tile, :tall, :] = kept[:, lanes]
        rows_ref[tile, tall:, :] = more[:, lanes]
    for tile in range(columns // 128):
        lanes = slice(tile * 128, tile * 128 + 128)
        for level in range(depth):
            own = rows_ref[tile, pl.ds(level, fields, stride=depth), :]
            out_ref[level, :first, lanes] = jnp.concatenate(
                [own, jnp.zeros((first - fields, 128), F32)], axis=0
            ).astype(BF16)
            more = rows_ref[tile, pl.ds(tall + level, extra, stride=depth), :]
            out_ref[level, first:, lanes] = jnp.concatenate(
                [more, jnp.zeros((64 - extra, 128), F32)], axis=0
            ).astype(BF16)


def base(me, map_row, dyn_state, aerosol):
    fields, levels, columns = dyn_state.shape
    extra = aerosol.shape[0]
    depth = 16
    return pl.pallas_call(
        base_kernel,
        grid=(levels // depth,),
        in_specs=[
            pl.BlockSpec(memory_space=pltpu.SMEM),
            pl.BlockSpec((1, columns), lambda i: (0, 0)),
            pl.BlockSpec((fields, depth, columns), lambda i: (0, i, 0)),
            pl.BlockSpec((extra, depth, columns), lambda i: (0, i, 0)),
        ],
        out_specs=pl.BlockSpec((depth, 112, columns), lambda i: (i, 0, 0)),
        out_shape=jax.ShapeDtypeStruct((levels, 112, columns), BF16),
        scratch_shapes=[
            pltpu.VMEM((columns, columns), BF16),
            pltpu.VMEM((columns // 128, (fields + extra) * depth, 128), F32),
        ],
        compiler_params=pltpu.CompilerParams(vmem_limit_bytes=48 * MIB),
        cost_estimate=pl.CostEstimate(
            flops=2 * fields * levels * columns * columns, bytes_accessed=14 * MIB, transcendentals=0
        ),
        name="base",
    )(me, map_row, dyn_state, aerosol)


def flux_kernel(
    recv_hbm,
    base_hbm,
    k_ref,
    planck_ref,
    solar_ref,
    side_ref,
    heat_ref,
    surface_ref,
    back_ref,
    recv_ref,
    field_ref,
    pick_ref,
    state_ref,
    warm_ref,
    trans_ref,
    down_ref,
    beam_ref,
    diff_ref,
    up_ref,
    spread_ref,
    net_lw_ref,
    net_sw_ref,
    sems,
):
    rows = recv_ref.shape[0]
    devices = rows // (2 * CAP)
    levels, depth, columns = field_ref.shape
    glw = planck_ref.shape[0]
    gsw = solar_ref.shape[0]
    span = trans_ref.shape[2]
    tall = state_ref.shape[1]
    fields = tall // 32

    recv_copy = pltpu.make_async_copy(recv_hbm, recv_ref, sems.at[0])
    base_copy = pltpu.make_async_copy(base_hbm, field_ref, sems.at[1])
    recv_copy.start()
    base_copy.start()

    recv_copy.wait()
    mark = recv_ref[:, tall : tall + 128].astype(F32)
    mark = (mark[:, 0:1] * 2.0 + mark[:, 1:2]).astype(jnp.int32)
    half_of = lax.broadcasted_iota(jnp.int32, (rows, 1), 0) % 2
    for half in range(2):
        key = jnp.where(half_of == half, mark, 0)
        for tile in range(0, columns, 128):
            lane = lax.broadcasted_iota(jnp.int32, (rows, 128), 1) + (tile + 1)
            pick_ref[:, half * columns + tile : half * columns + tile + 128] = onehot(key == lane)
    for tile in range(0, tall, 128):
        moved = lax.dot_general(
            recv_ref[:, tile : tile + 128], pick_ref[...], TN, preferred_element_type=F32
        )
        for part in range(2 * columns // 128):
            state_ref[part, tile : tile + 128, :] = moved[:, part * 128 : part * 128 + 128]
    base_copy.wait()

    for half in range(2):

        def place_level(inner, _, half=half):
            level = half * 32 + inner
            here = jnp.concatenate(
                [
                    state_ref[half * (columns // 128) + part, pl.ds(inner, fields, stride=32), :]
                    for part in range(columns // 128)
                ],
                axis=1,
            )
            here = here + field_ref[level, :48, :].astype(F32)[:fields]
            warmth = softplus2(jnp.broadcast_to(here[0:1], (8, columns)) * LOG2E)
            warm_ref[level] = warmth * (1.0 / LOG2E)
            field_ref[level, :48, :] = jnp.concatenate(
                [here, jnp.zeros((48 - fields, columns), F32)], axis=0
            ).astype(BF16)
            return 0

        lax.fori_loop(0, 32, place_level, 0)

    side = side_ref[...]
    cosine, albedo, ground, lit = (side[i : i + 1] for i in range(4))
    slant = (-SW_DEPTH / levels) / cosine
    skin = softplus2(ground * LOG2E) * (1.0 / LOG2E)
    tiles = span // 128
    for start in range(0, columns, span):
        lanes = [slice(start + 128 * t, start + 128 * t + 128) for t in range(tiles)]
        cuts = [slice(128 * t, 128 * t + 128) for t in range(tiles)]
        down_ref[0] = jnp.zeros((glw, span), F32)
        spread_ref[...] = jnp.zeros((gsw, span), F32)
        for t in range(tiles):
            beam_ref[0, :, cuts[t]] = SCATTER * solar_ref[...]

        def descend(level, _):
            depth_of = jnp.dot(
                k_ref[...], field_ref[level, :, start : start + span], preferred_element_type=F32
            )
            for t in range(tiles):
                warm = warm_ref[level, :, lanes[t]]
                slope = jnp.broadcast_to(slant[:, lanes[t]], (8, 128))
                for g in range(0, glw, 8):
                    u = depth_of[g : g + 8, cuts[t]] * LOG2E
                    tau = jnp.log2(1.0 + jnp.exp2(jnp.minimum(u, 126.0)))
                    trans = jnp.exp2(tau * (-DIFFUSE))
                    trans_ref[level, g : g + 8, cuts[t]] = trans
                    down = down_ref[level, g : g + 8, cuts[t]]
                    down_ref[level + 1, g : g + 8, cuts[t]] = warm + trans * (down - warm)
                sum_beam = jnp.zeros((8, 128), F32)
                sum_spread = jnp.zeros((8, 128), F32)
                for g in range(0, gsw, 8):
                    u = depth_of[glw + g : glw + g + 8, cuts[t]] * LOG2E
                    tau = jnp.maximum(u, jnp.log2(1.0 + jnp.exp2(jnp.minimum(u, 126.0))))
                    direct = jnp.exp2(tau * slope)
                    diffuse = jnp.exp2(tau * (-DIFFUSE * SW_DEPTH / levels))
                    diff_ref[level, g : g + 8, cuts[t]] = diffuse
                    beam = beam_ref[level, g : g + 8, cuts[t]]
                    lower = direct * beam
                    beam_ref[level + 1, g : g + 8, cuts[t]] = lower
                    spread = spread_ref[g : g + 8, cuts[t]]
                    spread_ref[g : g + 8, cuts[t]] = diffuse * spread + (beam - lower)
                    sum_beam = sum_beam + beam
                    sum_spread = sum_spread + spread
                net_sw_ref[level, :, lanes[t]] = sum_beam * (1.0 / SCATTER) + sum_spread
            return 0

        lax.fori_loop(0, levels, descend, 0)

        for t in range(tiles):
            sum_net = jnp.zeros((8, 128), F32)
            ground_up = jnp.broadcast_to(skin[:, lanes[t]], (8, 128))
            sum_floor = jnp.zeros((8, 128), F32)
            for g in range(0, glw, 8):
                floor = planck_ref[g : g + 8, :] * down_ref[levels, g : g + 8, cuts[t]]
                sum_floor = sum_floor + floor
                sum_net = sum_net + (floor - planck_ref[g : g + 8, :] * ground_up)
                up_ref[g : g + 8, cuts[t]] = ground_up
            net_lw_ref[levels, :, lanes[t]] = sum_net
            surface_ref[0:1, lanes[t]] = jnp.sum(sum_floor, axis=0, keepdims=True) * (1.0 / glw)
            bright = jnp.broadcast_to(albedo[:, lanes[t]], (8, 128))
            sum_floor = jnp.zeros((8, 128), F32)
            for g in range(0, gsw, 8):
                floor = beam_ref[levels, g : g + 8, cuts[t]] * (1.0 / SCATTER) + spread_ref[g : g + 8, cuts[t]]
                sum_floor = sum_floor + floor
                spread_ref[g : g + 8, cuts[t]] = bright * floor
            net_sw_ref[levels, :, lanes[t]] = sum_floor - bright * sum_floor
            surface_ref[1:2, lanes[t]] = jnp.sum(sum_floor, axis=0, keepdims=True) * (
                lit[:, lanes[t]] * cosine[:, lanes[t]] * (1.0 / gsw)
            )

        def ascend(step, _):
            level = levels - 1 - step
            for t in range(tiles):
                warm = warm_ref[level, :, lanes[t]]
                sum_net = jnp.zeros((8, 128), F32)
                for g in range(0, glw, 8):
                    upper = warm + trans_ref[level, g : g + 8, cuts[t]] * (up_ref[g : g + 8, cuts[t]] - warm)
                    up_ref[g : g + 8, cuts[t]] = upper
                    sum_net = sum_net + planck_ref[g : g + 8, :] * (
                        down_ref[level, g : g + 8, cuts[t]] - upper
                    )
                net_lw_ref[level, :, lanes[t]] = sum_net
                sum_up = jnp.zeros((8, 128), F32)
                for g in range(0, gsw, 8):
                    upper = diff_ref[level, g : g + 8, cuts[t]] * spread_ref[g : g + 8, cuts[t]] + (
                        beam_ref[level, g : g + 8, cuts[t]] - beam_ref[level + 1, g : g + 8, cuts[t]]
                    )
                    spread_ref[g : g + 8, cuts[t]] = upper
                    sum_up = sum_up + upper
                net_sw_ref[level, :, lanes[t]] = net_sw_ref[level, :, lanes[t]] - sum_up
            return 0

        lax.fori_loop(0, levels, ascend, 0)

    net_lw = jnp.sum(net_lw_ref[...], axis=1)
    net_sw = jnp.sum(net_sw_ref[...], axis=1)
    heat = (net_lw[:levels] - net_lw[1 : levels + 1]) * (1.0 / glw) + (
        net_sw[:levels] - net_sw[1 : levels + 1]
    ) * (lit * cosine * (1.0 / gsw))
    heat_ref[...] = heat

    twice = jnp.concatenate([heat, heat], axis=0)
    high, low = halves(twice)
    picked = pick_ref[:, :columns]
    state_ref[0, :rows, :] = lax.dot_general(picked, high, NT, preferred_element_type=F32) + lax.dot_general(
        picked, low, NT, preferred_element_type=F32
    )
    left = lax.broadcasted_iota(jnp.int32, (devices, 128), 1) < levels
    for pair in range(2):
        even = state_ref[0, pl.ds(4 * pair, devices, stride=8), :]
        odd = state_ref[0, pl.ds(4 * pair + 2, devices, stride=8), :]
        back_ref[pl.ds(pair, devices, stride=2), :] = jnp.where(left, even, odd)


def flux(recv, fields_base, coefficients, planck, solar, side, fields):
    rows, width = recv.shape
    levels, depth, columns = fields_base.shape
    glw, gsw = planck.shape[0], solar.shape[0]
    span = 256
    devices = rows // (2 * CAP)
    whole = pl.BlockSpec(memory_space=pltpu.VMEM)
    count = (glw + gsw) * levels * columns
    return pl.pallas_call(
        flux_kernel,
        in_specs=[pl.BlockSpec(memory_space=pl.ANY)] * 2 + [whole] * 4,
        out_specs=[whole] * 3,
        out_shape=[
            jax.ShapeDtypeStruct((levels, columns), F32),
            jax.ShapeDtypeStruct((2, columns), F32),
            jax.ShapeDtypeStruct((devices * 2, 128), F32),
        ],
        scratch_shapes=[
            pltpu.VMEM((rows, width), BF16),
            pltpu.VMEM((levels, depth, columns), BF16),
            pltpu.VMEM((rows, 2 * columns), BF16),
            pltpu.VMEM((2 * columns // 128, fields * 32, 128), F32),
            pltpu.VMEM((levels, 8, columns), F32),
            pltpu.VMEM((levels, glw, span), F32),
            pltpu.VMEM((levels + 1, glw, span), F32),
            pltpu.VMEM((levels + 1, gsw, span), F32),
            pltpu.VMEM((levels, gsw, span), F32),
            pltpu.VMEM((glw, span), F32),
            pltpu.VMEM((gsw, span), F32),
            pltpu.VMEM((levels + 1, 8, columns), F32),
            pltpu.VMEM((levels + 1, 8, columns), F32),
            pltpu.SemaphoreType.DMA((2,)),
        ],
        compiler_params=pltpu.CompilerParams(vmem_limit_bytes=58 * MIB),
        cost_estimate=pl.CostEstimate(flops=250 * count, bytes_accessed=12 * MIB, transcendentals=4 * count),
        name="flux",
    )(recv, fields_base, coefficients, planck, solar, side)


def local_kernel(me_ref, map_ref, heat_ref, out_ref):
    columns = map_ref.shape[1]
    goal = lax.broadcasted_iota(jnp.int32, (columns, columns), 0) + me_ref[0] * columns
    stay = onehot(map_ref[...] == goal)
    high, low = halves(heat_ref[...])
    out_ref[...] = jnp.dot(high, stay, preferred_element_type=F32) + jnp.dot(
        low, stay, preferred_element_type=F32
    )


def unpack_kernel(local_ref, pick_ref, back_ref, out_ref):
    devices = back_ref.shape[0] // 2
    levels = local_ref.shape[0]
    total = local_ref[...]
    for pair in range(2):
        high, low = halves(back_ref[pl.ds(pair, devices, stride=2), :])
        for side in range(2):
            place = 2 * pair + side
            pick = pick_ref[place * devices : (place + 1) * devices, :]
            part = lax.dot_general(high, pick, TN, preferred_element_type=F32) + lax.dot_general(
                low, pick, TN, preferred_element_type=F32
            )
            total = total + part[side * levels : (side + 1) * levels]
    out_ref[...] = total


def shards(
    dyn_state,
    span_map,
    sunlit,
    coszen,
    albedo,
    ground_temp,
    aerosol,
    k_long,
    planck,
    k_short,
    solar_flux,
):
    fields, levels, columns = dyn_state.shape
    devices = lax.axis_size("gx") * lax.axis_size("gy")
    me = lax.axis_index(AXES).astype(jnp.int32).reshape(1)
    map_row = span_map.reshape(1, columns)
    swap = functools.partial(lax.all_to_all, axis_name=AXES, split_axis=0, concat_axis=0, tiled=True)

    outgoing, pick = pack(me, map_row, dyn_state, devices)
    width = outgoing.shape[1]
    recv = swap(outgoing.reshape(devices, 2 * CAP, width)).reshape(devices * 2 * CAP, width)
    fields_base = base(me, map_row, dyn_state, aerosol)

    both = jnp.concatenate([k_long, k_short], axis=0)
    gap = lambda n: jnp.zeros((both.shape[0], n), both.dtype)
    coefficients = jnp.concatenate(
        [both[:, :fields], gap(48 - fields), both[:, fields:], gap(64 - aerosol.shape[0])], axis=1
    )
    side = jnp.stack([coszen, albedo, ground_temp, sunlit.astype(F32)], axis=0)
    wide = lambda x: jnp.broadcast_to(x[:, None], (x.shape[0], 128))
    heat, surface, back = flux(
        recv, fields_base, coefficients, wide(planck), wide(solar_flux), side, fields
    )

    returned = swap(back.reshape(devices, 2, 128)).reshape(devices * 2, 128)
    whole = pl.BlockSpec(memory_space=pltpu.VMEM)
    local = pl.pallas_call(
        local_kernel,
        in_specs=[pl.BlockSpec(memory_space=pltpu.SMEM), whole, whole],
        out_specs=whole,
        out_shape=jax.ShapeDtypeStruct((levels, columns), F32),
        cost_estimate=pl.CostEstimate(
            flops=4 * levels * columns * columns, bytes_accessed=MIB, transcendentals=0
        ),
        name="local",
    )(me, map_row, heat)
    heating = pl.pallas_call(
        unpack_kernel,
        in_specs=[whole] * 3,
        out_specs=whole,
        out_shape=jax.ShapeDtypeStruct((levels, columns), F32),
        cost_estimate=pl.CostEstimate(
            flops=8 * levels * columns * columns, bytes_accessed=MIB, transcendentals=0
        ),
        name="unpack",
    )(local, pick, returned)
    return heating, surface


def solution(mesh):
    cols = P(AXES)
    in_specs = (
        P(None, None, AXES),
        cols,
        cols,
        cols,
        cols,
        cols,
        P(None, None, AXES),
        P(),
        P(),
        P(),
        P(),
    )
    out_specs = (P(None, AXES), P(None, AXES))
    return jax.shard_map(shards, mesh=mesh, in_specs=in_specs, out_specs=out_specs, check_vma=False)
```

profile of v0, /device:TPU:1, one launch (start us, length us, event | category | flops | bytes accessed | tf_op | source)
XLA Modules:
  0.0 137.0 jit_solution(13654242820957229254)
XLA Ops:
  0.6 0.0 copy-start
  0.6 1.7 %copy-done = bf16[40,64,512]{2,1,0:T(8,128)(2,1)S(1)} copy-done((bf16[40,64,512]{2,1,0:T(8,128)(2,1)S(1)}, bf16[40,64,512]{2,1,0:T(8,128)(2,1)}, u32[]{:S(2)}) %copy-start) | copy-done | bytes 2621464
  2.4 0.0 copy-start.3
  2.4 0.7 copy-done.3
  3.1 7.6 %pack.1 = (bf16[1024,1408]{1,0:T(8,128)(2,1)}, bf16[512,512]{1,0:T(8,128)(2,1)S(1)}) custom-call(s32[1]{0:T(128)} %bitcast.me_ref, s32[1,512]{1,0:T(1,128)S(1)} %bitcast.11, bf16[40,64,512]{2,1,0:T(8,128)(2,1)S(1)} %copy-done), custom_call_target="tpu_custom_call" | custom-call | flops 1342177280 | bytes 6291456 | tf_op jit(solution)/shard_map/pack/pallas_call | solution.py:85
  10.6 0.0 copy-start.2
  10.6 0.8 copy-done.2
  11.4 0.0 copy-start.8
  11.4 0.0 copy-start.6
  11.4 0.0 copy-start.7
  11.4 0.0 copy-start.9
  11.4 0.0 copy-start.10
  11.5 0.0 copy-start.11
  11.5 0.0 copy-start.1
  11.5 0.0 copy-start.4
  11.5 11.9 %all-to-all-start = ((bf16[128,8,1408]{2,1,0:T(8,128)(2,1)}), bf16[128,8,1408]{2,1,0:T(8,128)(2,1)}, u32[]{:S(2)}, u32[]{:S(2)}) async-start(bf16[128,8,1408]{2,1,0:T(8,128)(2,1)} %bitcast.2), calls=%async_computation | async-start | bytes 5767168 | tf_op jit(solution)/shard_map/all_to_all | solution.py:448
  23.4 0.1 pad.7.clone
  23.5 0.1 pad.5.clone
  23.6 0.0 copy-done.8
  23.6 0.0 copy-done.6
  23.6 0.1 copy.14
  23.7 0.0 copy-done.7
  23.7 0.1 copy.13
  23.8 0.0 copy-done.9
  23.8 0.0 copy-done.10
  23.8 0.0 copy-done.11
  23.9 0.6 pad_maximum_fusion.side_ref
  24.5 0.0 copy-done.1
  24.5 0.0 copy-done.4
  24.5 0.0 copy-start.12
  24.5 0.0 copy-start.13
  24.5 9.7 %base.1.base_hbm = bf16[64,112,512]{2,1,0:T(8,128)(2,1)} custom-call(s32[1]{0:T(128)} %bitcast.me_ref, s32[1,512]{1,0:T(1,128)S(1)} %bitcast.12, bf16[40,64,512]{2,1,0:T(8,128)(2,1)S(1)} %copy-done.1, bf16[58,64,512]{2,1,0:T(8,128)(2,1)} %aer_ref.1), custom_call_target="tpu_custom_call" | custom-call | flops 1342177280 | bytes 14680064 | tf_op jit(solution)/shard_map/base/pallas_call | solution.py:149
  34.2 0.7 fusion.5.k_ref
  35.0 26.3 %all-to-all-done = bf16[128,8,1408]{2,1,0:T(8,128)(2,1)} async-done(((bf16[128,8,1408]{2,1,0:T(8,128)(2,1)}), bf16[128,8,1408]{2,1,0:T(8,128)(2,1)}, u32[]{:S(2)}, u32[]{:S(2)}) %all-to-all-start) | async-done | bytes 2883616 | tf_op jit(solution)/shard_map/all_to_all | solution.py:448
  61.2 0.0 copy-done.12
  61.3 0.7 broadcast_in_dim.21.solar_ref
  61.9 0.0 copy-done.13
  62.0 0.7 broadcast_in_dim.20.planck_ref
  62.6 56.6 %flux.1 = (f32[64,512]{1,0:T(8,128)}, f32[2,512]{1,0:T(2,128)}, f32[256,128]{1,0:T(8,128)}) custom-call(bf16[1024,1408]{1,0:T(8,128)(2,1)} %bitcast.3.recv_hbm, bf16[64,112,512]{2,1,0:T(8,128)(2,1)} %base.1.base_hbm, bf16[240,112]{1,0:T(8,128)(2,1)} %fusion.5.k_ref, f32[128,128]{1,0:T(8,128)} %broadcast_in_dim.20.planck_ref, ...), custom_call_target="tpu_custom_call" | custom-call | flops 1966080000 | bytes 12582912 | tf_op jit(solution)/shard_map/flux/pallas_call | solution.py:370
  119.2 4.8 %all-to-all-start.1 = ((f32[128,2,128]{2,1,0:T(2,128)}), f32[128,2,128]{2,1,0:T(2,128)S(1)}, u32[]{:S(2)}, u32[]{:S(2)}) async-start(f32[128,2,128]{2,1,0:T(2,128)} %bitcast.14), calls=%async_computation.1 | async-start | bytes 262144 | tf_op jit(solution)/shard_map/all_to_all | solution.py:462
  124.0 1.9 %local.1.local_ref = f32[64,512]{1,0:T(8,128)} custom-call(s32[1]{0:T(128)} %bitcast.me_ref, s32[1,512]{1,0:T(1,128)} %bitcast.10, f32[64,512]{1,0:T(8,128)} %get-tuple-element.8.heat_ref), custom_call_target="tpu_custom_call" | custom-call | flops 67108864 | bytes 1048576 | tf_op jit(solution)/shard_map/local/pallas_call | solution.py:464
  125.9 8.2 %all-to-all-done.1 = f32[128,2,128]{2,1,0:T(2,128)S(1)} async-done(((f32[128,2,128]{2,1,0:T(2,128)}), f32[128,2,128]{2,1,0:T(2,128)S(1)}, u32[]{:S(2)}, u32[]{:S(2)}) %all-to-all-start.1) | async-done | bytes 131104 | tf_op jit(solution)/shard_map/all_to_all | solution.py:462
  134.1 0.0 copy-start.5
  134.1 0.6 copy-done.5
  134.7 2.2 %unpack.1 = f32[64,512]{1,0:T(8,128)} custom-call(f32[64,512]{1,0:T(8,128)} %local.1.local_ref, bf16[512,512]{1,0:T(8,128)(2,1)} %copy-done.2, f32[256,128]{1,0:T(8,128)} %bitcast.13), custom_call_target="tpu_custom_call" | custom-call | flops 134217728 | bytes 1048576 | tf_op jit(solution)/shard_map/unpack/pallas_call | solution.py:474
  (4 shorter events, 0.0 us)
Async XLA Ops:
  0.6 1.7 %copy-start = (bf16[40,64,512]{2,1,0:T(8,128)(2,1)S(1)}, bf16[40,64,512]{2,1,0:T(8,128)(2,1)}, u32[]{:S(2)}) copy-start(bf16[40,64,512]{2,1,0:T(8,128)(2,1)} %dyn_ref.3) | copy-start | bytes 7864324
  2.4 0.7 copy-start.3
  10.6 0.8 copy-start.2
  11.4 12.1 %copy-start.8 = (s32[512]{0:T(512)S(1)}, s32[512]{0:T(512)}, u32[]{:S(2)}) copy-start(s32[512]{0:T(512)} %param.13) | copy-start | bytes 6148
  11.4 12.1 %copy-start.6 = (bf16[112,98]{0,1:T(8,128)(2,1)S(1)}, bf16[112,98]{0,1:T(8,128)(2,1)}, u32[]{:S(2)}) copy-start(bf16[112,98]{0,1:T(8,128)(2,1)} %param.20) | copy-start | bytes 65860
  11.4 12.3 %copy-start.7 = (bf16[128,98]{0,1:T(8,128)(2,1)S(1)}, bf16[128,98]{0,1:T(8,128)(2,1)}, u32[]{:S(2)}) copy-start(bf16[128,98]{0,1:T(8,128)(2,1)} %param.18) | copy-start | bytes 75268
  11.4 12.4 %copy-start.9 = (f32[512]{0:T(512)S(1)}, f32[512]{0:T(512)}, u32[]{:S(2)}) copy-start(f32[512]{0:T(512)} %param.16) | copy-start | bytes 6148
  11.4 12.4 %copy-start.10 = (f32[512]{0:T(512)S(1)}, f32[512]{0:T(512)}, u32[]{:S(2)}) copy-start(f32[512]{0:T(512)} %param.15) | copy-start | bytes 6148
  11.5 12.4 %copy-start.11 = (f32[512]{0:T(512)S(1)}, f32[512]{0:T(512)}, u32[]{:S(2)}) copy-start(f32[512]{0:T(512)} %param.14) | copy-start | bytes 6148
  11.5 13.0 %copy-start.1 = (bf16[40,64,512]{2,1,0:T(8,128)(2,1)S(1)}, bf16[40,64,512]{2,1,0:T(8,128)(2,1)}, u32[]{:S(2)}) copy-start(bf16[40,64,512]{2,1,0:T(8,128)(2,1)} %dyn_ref.3) | copy-start | bytes 7864324
  11.5 13.0 %copy-start.4 = (s32[512]{0:T(512)S(1)}, s32[512]{0:T(512)}, u32[]{:S(2)}) copy-start(s32[512]{0:T(512)} %param.12) | copy-start | bytes 6148
  11.5 49.8 %all-to-all-start = ((bf16[128,8,1408]{2,1,0:T(8,128)(2,1)}), bf16[128,8,1408]{2,1,0:T(8,128)(2,1)}, u32[]{:S(2)}, u32[]{:S(2)}) async-start(bf16[128,8,1408]{2,1,0:T(8,128)(2,1)} %bitcast.2), calls=%async_computation | async-start | bytes 5767168 | tf_op jit(solution)/shard_map/all_to_all | solution.py:448
  24.5 36.7 %copy-start.12 = (f32[112]{0:T(128)S(1)}, f32[112]{0:T(128)}, u32[]{:S(2)}) copy-start(f32[112]{0:T(128)} %param.21) | copy-start | bytes 1348
  24.5 37.4 %copy-start.13 = (f32[128]{0:T(128)S(1)}, f32[128]{0:T(128)}, u32[]{:S(2)}) copy-start(f32[128]{0:T(128)} %param.19) | copy-start | bytes 1540
  119.2 14.9 %all-to-all-start.1 = ((f32[128,2,128]{2,1,0:T(2,128)}), f32[128,2,128]{2,1,0:T(2,128)S(1)}, u32[]{:S(2)}, u32[]{:S(2)}) async-start(f32[128,2,128]{2,1,0:T(2,128)} %bitcast.14), calls=%async_computation.1 | async-start | bytes 262144 | tf_op jit(solution)/shard_map/all_to_all | solution.py:462
  134.1 0.6 copy-start.5
where the time goes:
time: 137 us
  Pallas kernels  78 us (57%)
  waiting for transfers between devices  34.5 us (25%)
  starting transfers between devices  16.7 us (12%)
  local copies, waits for them, and re-layouts  5.7 us (4%)
    pallas_call x1, Pallas kernels, flux(): pl.pallas_call(flux_kernel, in_specs=[pl.BlockSpec(memory_space=pl.ANY)]...  56.6 us
    all_to_all x1, waiting for transfers between devices, shards(): swap(outgoing.reshape(devices, 2 * CAP, width))  26.3 us
    all_to_all x1, starting transfers between devices, shards(): swap(outgoing.reshape(devices, 2 * CAP, width))  11.9 us
    pallas_call x1, Pallas kernels, base(): pl.pallas_call(base_kernel, grid=(levels // depth,), in_specs=[pl.BlockSp...  9.71 us
    all_to_all x1, waiting for transfers between devices, shards(): returned = swap(back.reshape(devices, 2, 128)).reshape(devices * 2, 128)  8.16 us
    pallas_call x1, Pallas kernels, pack(): pl.pallas_call(pack_kernel, grid=(steps + 1,), in_specs=[pl.BlockSpec(mem...  7.57 us
    all_to_all x1, starting transfers between devices, shards(): returned = swap(back.reshape(devices, 2, 128)).reshape(devices * 2, 128)  4.8 us
    unnamed x30, local copies, waits for them, and re-layouts  4.14 us
  transfers between devices with their start and end apart: 2, of which 2 were waited for; matrix products, arithmetic and copies ran while one was open for 1% of the time, Pallas kernels for 8%

commit v1 on v0

v1 whole, which is shorter than its diff:
```python
import functools

import jax
import jax.numpy as jnp
from jax import lax
from jax.experimental import pallas as pl
from jax.experimental.pallas import tpu as pltpu
from jax.sharding import PartitionSpec as P

AXES = ("gx", "gy")
DIFFUSE = 1.66
SCATTER = 0.3
SW_DEPTH = 2.0
LOG2E = 1.4426950408889634
CAP = 4
BF16 = jnp.bfloat16
F32 = jnp.float32
NT = (((1,), (1,)), ((), ()))
TN = (((0,), (0,)), ((), ()))
MIB = 1 << 20


def onehot(mask):
    return jnp.where(mask, 1.0, 0.0).astype(BF16)


def halves(x):
    high = x.astype(BF16)
    return high, (x - high.astype(F32)).astype(BF16)


def softplus2(u):
    return jnp.maximum(u, jnp.log2(1.0 + jnp.exp2(jnp.minimum(u, 126.0))))


def pack_kernel(me_ref, map_ref, dyn_ref, out_ref, pick_ref, meta_ref, rows_ref):
    devices = out_ref.shape[0] // (2 * CAP)
    columns = map_ref.shape[1]
    step = pl.program_id(0)
    last = pl.num_programs(0) - 1

    @pl.when(step == 0)
    def _():
        where_to = map_ref[...]
        target = where_to // columns
        slot = where_to % columns
        same = target == lax.broadcasted_iota(jnp.int32, (devices, columns), 0)
        earlier = onehot(
            lax.broadcasted_iota(jnp.int32, (columns, columns), 0)
            < lax.broadcasted_iota(jnp.int32, (columns, columns), 1)
        )
        before = jnp.dot(onehot(same), earlier, preferred_element_type=F32)
        rank = jnp.sum(jnp.where(same, before, 0.0), axis=0, keepdims=True).astype(jnp.int32)
        rank = jnp.where(target == me_ref[0], CAP, rank)
        for place in range(CAP):
            pick_ref[place * devices : (place + 1) * devices, :] = onehot(same & (rank == place))
        line = lax.broadcasted_iota(jnp.int32, (128, columns), 0)
        mark = slot + 1
        meta = jnp.where(line == 0, mark // 2, jnp.where(line == 1, mark % 2, 0))
        meta_ref[...] = meta.astype(F32).astype(BF16)

    def put(part, half):
        moved = lax.dot_general(pick_ref[...], part, NT, preferred_element_type=F32)
        for place in range(CAP):
            rows_ref[pl.ds(place * 2 + half, devices, stride=2 * CAP), :] = moved[
                place * devices : (place + 1) * devices
            ]

    @pl.when(step < last)
    def _():
        for half in range(2):
            put(dyn_ref[:, half * 32 : half * 32 + 32, :].reshape(128, columns), half)

    @pl.when(step == last)
    def _():
        for half in range(2):
            put(meta_ref[...], half)

    out_ref[...] = rows_ref[...].astype(BF16)


def pack(me, map_row, dyn_state, devices):
    fields, levels, columns = dyn_state.shape
    steps = fields // 4
    return pl.pallas_call(
        pack_kernel,
        grid=(steps + 1,),
        in_specs=[
            pl.BlockSpec(memory_space=pltpu.SMEM),
            pl.BlockSpec((1, columns), lambda i: (0, 0)),
            pl.BlockSpec((4, levels, columns), lambda i: (jnp.minimum(i, steps - 1), 0, 0)),
        ],
        out_specs=[
            pl.BlockSpec((devices * CAP * 2, 128), lambda i: (0, i)),
            pl.BlockSpec((devices * CAP, columns), lambda i: (0, 0)),
        ],
        out_shape=[
            jax.ShapeDtypeStruct((devices * CAP * 2, (steps + 1) * 128), BF16),
            jax.ShapeDtypeStruct((devices * CAP, columns), BF16),
        ],
        scratch_shapes=[
            pltpu.VMEM((128, columns), BF16),
            pltpu.VMEM((devices * CAP * 2, 128), F32),
        ],
        compiler_params=pltpu.CompilerParams(vmem_limit_bytes=56 * MIB),
        cost_estimate=pl.CostEstimate(
            flops=2 * fields * levels * columns * devices * CAP, bytes_accessed=6 * MIB, transcendentals=0
        ),
        name="pack",
    )(me, map_row, dyn_state)


def base_kernel(
    me_ref,
    map_ref,
    dyn_ref,
    aer_ref,
    long_ref,
    short_ref,
    planck_ref,
    solar_ref,
    out_ref,
    warm_ref,
    k_ref,
    weight_ref,
    pick_ref,
    rows_ref,
):
    fields, depth, columns = dyn_ref.shape
    extra = aer_ref.shape[0]
    tiles = columns // 128
    first = 48
    glw, gsw = long_ref.shape[0], short_ref.shape[0]

    @pl.when(pl.program_id(0) == 0)
    def _():
        goal = lax.broadcasted_iota(jnp.int32, (columns, columns), 0) + me_ref[0] * columns
        pick_ref[...] = onehot(map_ref[...] == goal)
        k_ref[...] = jnp.zeros(k_ref.shape, BF16)
        for coefficients, start in ((long_ref[...], 0), (short_ref[...], glw)):
            rows = slice(start, start + coefficients.shape[0])
            k_ref[rows, :fields] = coefficients[:, :fields]
            k_ref[rows, 48 : 48 + fields] = coefficients[:, :fields]
            k_ref[rows, 96 : 96 + extra] = coefficients[:, fields:]
        square = lax.broadcasted_iota(jnp.int32, (128, 128), 0) == lax.broadcasted_iota(
            jnp.int32, (128, 128), 1
        )
        for source, start in ((planck_ref[...], 0), (solar_ref[...], glw)):
            size = source.shape[1]
            picked = jnp.where(square[:size, :size], source, 0.0)
            weight_ref[start : start + size, :] = jnp.broadcast_to(
                jnp.sum(picked, axis=1, keepdims=True), (size, 128)
            )

    kept = lax.dot_general(
        dyn_ref[...].reshape(fields * depth, columns), pick_ref[...], NT, preferred_element_type=F32
    )
    warm_ref[...] = kept[:depth]
    tall = fields * depth
    more = aer_ref[...].reshape(extra * depth, columns).astype(F32)
    for tile in range(tiles):
        lanes = slice(tile * 128, tile * 128 + 128)
        rows_ref[tile, :tall, :] = kept[:, lanes]
        rows_ref[tile, tall:, :] = more[:, lanes]
    for tile in range(tiles):
        for level in range(depth):
            own = rows_ref[tile, pl.ds(level, fields, stride=depth), :]
            out_ref[tile, level, :first, :] = jnp.concatenate(
                [own, jnp.zeros((first - fields, 128), F32)], axis=0
            ).astype(BF16)
            aero = rows_ref[tile, pl.ds(tall + level, extra, stride=depth), :]
            out_ref[tile, level, first:, :] = jnp.concatenate(
                [aero, jnp.zeros((64 - extra, 128), F32)], axis=0
            ).astype(BF16)


def base(me, map_row, dyn_state, aerosol, k_long, k_short, planck, solar):
    fields, levels, columns = dyn_state.shape
    extra = aerosol.shape[0]
    glw, gsw = k_long.shape[0], k_short.shape[0]
    depth = 16
    tiles = columns // 128
    fixed = lambda *shape: pl.BlockSpec(shape, lambda i: (0,) * len(shape))
    return pl.pallas_call(
        base_kernel,
        grid=(levels // depth,),
        in_specs=[
            pl.BlockSpec(memory_space=pltpu.SMEM),
            fixed(1, columns),
            pl.BlockSpec((fields, depth, columns), lambda i: (0, i, 0)),
            pl.BlockSpec((extra, depth, columns), lambda i: (0, i, 0)),
            fixed(*k_long.shape),
            fixed(*k_short.shape),
            fixed(1, glw),
            fixed(1, gsw),
        ],
        out_specs=[
            pl.BlockSpec((tiles, depth, 112, 128), lambda i: (0, i, 0, 0)),
            pl.BlockSpec((depth, columns), lambda i: (i, 0)),
            fixed(glw + gsw, 160),
            fixed(glw + gsw, 128),
        ],
        out_shape=[
            jax.ShapeDtypeStruct((tiles, levels, 112, 128), BF16),
            jax.ShapeDtypeStruct((levels, columns), F32),
            jax.ShapeDtypeStruct((glw + gsw, 160), BF16),
            jax.ShapeDtypeStruct((glw + gsw, 128), F32),
        ],
        scratch_shapes=[
            pltpu.VMEM((columns, columns), BF16),
            pltpu.VMEM((tiles, (fields + extra) * depth, 128), F32),
        ],
        compiler_params=pltpu.CompilerParams(vmem_limit_bytes=56 * MIB),
        cost_estimate=pl.CostEstimate(
            flops=2 * fields * levels * columns * columns, bytes_accessed=14 * MIB, transcendentals=0
        ),
        name="base",
    )(me, map_row, dyn_state, aerosol, k_long, k_short, planck.reshape(1, glw), solar.reshape(1, gsw))


def flux_kernel(
    recv_hbm,
    base_hbm,
    kept_ref,
    k_ref,
    weight_ref,
    cos_ref,
    albedo_ref,
    ground_ref,
    lit_ref,
    heat_ref,
    surface_ref,
    back_ref,
    recv_ref,
    base_ref,
    pick_ref,
    state_ref,
    warm_ref,
    trans_refs,
    down_refs,
    beam_refs,
    diff_refs,
    depth_refs,
    up_ref,
    spread_ref,
    return_ref,
    net_lw_ref,
    net_sw_ref,
    sems,
):
    rows = recv_ref.shape[0]
    devices = rows // (2 * CAP)
    tiles, levels, _, _ = base_ref.shape
    columns = 128 * tiles
    glw, gsw = up_ref.shape[0], return_ref.shape[0]
    tall = state_ref.shape[1]
    fields = tall // 32
    pairs = levels // 2

    recv_copy = pltpu.make_async_copy(recv_hbm, recv_ref, sems.at[0])
    base_copy = pltpu.make_async_copy(base_hbm, base_ref, sems.at[1])
    recv_copy.start()
    base_copy.start()

    recv_copy.wait()
    mark = recv_ref[:, tall : tall + 128].astype(F32)
    mark = (mark[:, 0:1] * 2.0 + mark[:, 1:2]).astype(jnp.int32)
    half_of = lax.broadcasted_iota(jnp.int32, (rows, 1), 0) % 2
    for half in range(2):
        key = jnp.where(half_of == half, mark, 0)
        for tile in range(0, columns, 128):
            lane = lax.broadcasted_iota(jnp.int32, (rows, 128), 1) + (tile + 1)
            pick_ref[:, half * columns + tile : half * columns + tile + 128] = onehot(key == lane)
    for tile in range(0, tall, 128):
        moved = lax.dot_general(
            recv_ref[:, tile : tile + 128], pick_ref[...], TN, preferred_element_type=F32
        )
        for part in range(2 * tiles):
            state_ref[part, tile : tile + 128, :] = moved[:, part * 128 : part * 128 + 128]

    for part in range(2 * tiles):
        half, tile = part // tiles, part % tiles
        lanes = slice(tile * 128, tile * 128 + 128)
        cold = state_ref[part, :32, :] + kept_ref[half * 32 : half * 32 + 32, lanes]
        warmth = softplus2(cold * LOG2E) * (1.0 / LOG2E)
        for inner in range(32):
            warm_ref[half * 32 + inner, :, lanes] = jnp.broadcast_to(warmth[inner : inner + 1], (8, 128))
    base_copy.wait()

    cosine, albedo, ground = cos_ref[...], albedo_ref[...], ground_ref[...]
    lit = lit_ref[...].astype(F32)
    slant = (-SW_DEPTH / levels) / cosine
    skin = softplus2(ground * LOG2E) * (1.0 / LOG2E)
    lanes_of = lambda tile: slice(tile * 128, tile * 128 + 128)

    def absorb(pair, tile):
        half = pair // (pairs // 2)
        inner = 2 * pair - 32 * half
        both = [
            state_ref[half * tiles + tile, pl.ds(inner + e, fields, stride=32), :] for e in range(2)
        ]
        here = jnp.concatenate(
            [jnp.concatenate(both, axis=1), jnp.zeros((48 - fields, 256), F32)], axis=0
        ).astype(BF16)
        rest = jnp.concatenate([base_ref[tile, 2 * pair + e] for e in range(2)], axis=1)
        return jnp.dot(k_ref[...], jnp.concatenate([here, rest], axis=0), preferred_element_type=F32)

    def descend(pair, tile, depth_ref):
        trans_ref, down_ref = trans_refs[tile % 2], down_refs[tile % 2]
        beam_ref, diff_ref = beam_refs[tile % 2], diff_refs[tile % 2]
        level = 2 * pair
        warm = [warm_ref[level + e, :, lanes_of(tile)] for e in range(2)]
        for g in range(0, glw, 8):
            down = down_ref[level, g : g + 8, :]
            for e in range(2):
                u = depth_ref[g : g + 8, 128 * e : 128 * e + 128] * LOG2E
                tau = jnp.log2(1.0 + jnp.exp2(jnp.minimum(u, 126.0)))
                trans = jnp.exp2(tau * (-DIFFUSE))
                trans_ref[level + e, g : g + 8, :] = trans
                down = warm[e] + trans * (down - warm[e])
                down_ref[level + e + 1, g : g + 8, :] = down
        slope = jnp.broadcast_to(slant[:, lanes_of(tile)], (8, 128))
        sum_beam = [jnp.zeros((8, 128), F32) for _ in range(2)]
        sum_spread = [jnp.zeros((8, 128), F32) for _ in range(2)]
        for g in range(0, gsw, 8):
            beam = beam_ref[level, g : g + 8, :]
            spread = spread_ref[g : g + 8, :]
            for e in range(2):
                u = depth_ref[glw + g : glw + g + 8, 128 * e : 128 * e + 128] * LOG2E
                tau = jnp.maximum(u, jnp.log2(1.0 + jnp.exp2(jnp.minimum(u, 126.0))))
                diffuse = jnp.exp2(tau * (-DIFFUSE * SW_DEPTH / levels))
                diff_ref[level + e, g : g + 8, :] = diffuse
                lower = jnp.exp2(tau * slope) * beam
                beam_ref[level + e + 1, g : g + 8, :] = lower
                sum_beam[e] = sum_beam[e] + beam
                sum_spread[e] = sum_spread[e] + spread
                spread = diffuse * spread + (beam - lower)
                beam = lower
            spread_ref[g : g + 8, :] = spread
        for e in range(2):
            net_sw_ref[level + e, :, lanes_of(tile)] = sum_beam[e] * (1.0 / SCATTER) + sum_spread[e]

    def ascend(pair, tile):
        trans_ref, down_ref = trans_refs[tile % 2], down_refs[tile % 2]
        beam_ref, diff_ref = beam_refs[tile % 2], diff_refs[tile % 2]
        level = 2 * pair
        warm = [warm_ref[level + e, :, lanes_of(tile)] for e in range(2)]
        total = [jnp.zeros((8, 128), F32) for _ in range(2)]
        for g in range(0, glw, 8):
            upper = up_ref[g : g + 8, :]
            weight = weight_ref[g : g + 8, :]
            for e in (1, 0):
                upper = warm[e] + trans_ref[level + e, g : g + 8, :] * (upper - warm[e])
                total[e] = total[e] + weight * (down_ref[level + e, g : g + 8, :] - upper)
            up_ref[g : g + 8, :] = upper
        for e in range(2):
            net_lw_ref[level + e, :, lanes_of(tile)] = total[e]
        total = [net_sw_ref[level + e, :, lanes_of(tile)] for e in range(2)]
        for g in range(0, gsw, 8):
            upper = return_ref[g : g + 8, :]
            lower = beam_ref[level + 2, g : g + 8, :]
            for e in (1, 0):
                beam = beam_ref[level + e, g : g + 8, :]
                upper = diff_ref[level + e, g : g + 8, :] * upper + (beam - lower)
                total[e] = total[e] - upper
                lower = beam
            return_ref[g : g + 8, :] = upper
        for e in range(2):
            net_sw_ref[level + e, :, lanes_of(tile)] = total[e]

    def turn(tile):
        lanes = lanes_of(tile)
        down_ref, beam_ref = down_refs[tile % 2], beam_refs[tile % 2]
        total = jnp.zeros((8, 128), F32)
        floor_total = jnp.zeros((8, 128), F32)
        upper = jnp.broadcast_to(skin[:, lanes], (8, 128))
        for g in range(0, glw, 8):
            weight = weight_ref[g : g + 8, :]
            floor = weight * down_ref[levels, g : g + 8, :]
            floor_total = floor_total + floor
            total = total + (floor - weight * upper)
            up_ref[g : g + 8, :] = upper
        net_lw_ref[levels, :, lanes] = total
        surface_ref[0:1, lanes] = jnp.sum(floor_total, axis=0, keepdims=True) * (1.0 / glw)
        bright = jnp.broadcast_to(albedo[:, lanes], (8, 128))
        floor_total = jnp.zeros((8, 128), F32)
        for g in range(0, gsw, 8):
            floor = beam_ref[levels, g : g + 8, :] * (1.0 / SCATTER) + spread_ref[g : g + 8, :]
            floor_total = floor_total + floor
            return_ref[g : g + 8, :] = bright * floor
        net_sw_ref[levels, :, lanes] = floor_total - bright * floor_total
        surface_ref[1:2, lanes] = jnp.sum(floor_total, axis=0, keepdims=True) * (
            lit[:, lanes] * cosine[:, lanes] * (1.0 / gsw)
        )

    depth_refs[0][...] = absorb(0, 0)
    for tile in range(tiles + 1):
        if tile < tiles:
            down_refs[tile % 2][0] = jnp.zeros((glw, 128), F32)
            spread_ref[...] = jnp.zeros((gsw, 128), F32)
            beam_refs[tile % 2][0] = SCATTER * weight_ref[glw:, :]

        def both_ways(step, _, tile=tile):
            for part in range(2):
                pair = 2 * step + part
                if tile < tiles:
                    over = pair == pairs - 1
                    following = jnp.where(over, 0, pair + 1)
                    following_tile = jnp.where(over, min(tile + 1, tiles - 1), tile)
                    depth_refs[1 - part][...] = absorb(following, following_tile)
                    descend(pair, tile, depth_refs[part])
                if tile > 0:
                    ascend(pairs - 1 - pair, tile - 1)
            return 0

        lax.fori_loop(0, pairs // 2, both_ways, 0, unroll=4)
        if tile < tiles:
            turn(tile)

    net_lw = jnp.sum(net_lw_ref[...], axis=1)
    net_sw = jnp.sum(net_sw_ref[...], axis=1)
    heat = (net_lw[:levels] - net_lw[1 : levels + 1]) * (1.0 / glw) + (
        net_sw[:levels] - net_sw[1 : levels + 1]
    ) * (lit * cosine * (1.0 / gsw))
    heat_ref[...] = heat

    twice = jnp.concatenate([heat, heat], axis=0)
    high, low = halves(twice)
    picked = pick_ref[:, :columns]
    state_ref[0, :rows, :] = lax.dot_general(picked, high, NT, preferred_element_type=F32) + lax.dot_general(
        picked, low, NT, preferred_element_type=F32
    )
    left = lax.broadcasted_iota(jnp.int32, (devices, 128), 1) < levels
    for pair in range(2):
        even = state_ref[0, pl.ds(4 * pair, devices, stride=8), :]
        odd = state_ref[0, pl.ds(4 * pair + 2, devices, stride=8), :]
        back_ref[pl.ds(pair, devices, stride=2), :] = jnp.where(left, even, odd)


def flux(recv, fields_base, kept, coefficients, weights, coszen, albedo, ground, sunlit, fields, glw):
    rows, width = recv.shape
    tiles, levels, depth, _ = fields_base.shape
    columns = 128 * tiles
    gsw = weights.shape[0] - glw
    devices = rows // (2 * CAP)
    whole = pl.BlockSpec(memory_space=pltpu.VMEM)
    count = (glw + gsw) * levels * columns
    twice = lambda *shape: [pltpu.VMEM(shape, F32)] * 2
    return pl.pallas_call(
        flux_kernel,
        in_specs=[pl.BlockSpec(memory_space=pl.ANY)] * 2 + [whole] * 7,
        out_specs=[whole] * 3,
        out_shape=[
            jax.ShapeDtypeStruct((levels, columns), F32),
            jax.ShapeDtypeStruct((2, columns), F32),
            jax.ShapeDtypeStruct((devices * 2, 128), F32),
        ],
        scratch_shapes=[
            pltpu.VMEM((rows, width), BF16),
            pltpu.VMEM((tiles, levels, depth, 128), BF16),
            pltpu.VMEM((rows, 2 * columns), BF16),
            pltpu.VMEM((2 * tiles, fields * 32, 128), F32),
            pltpu.VMEM((levels, 8, columns), F32),
            twice(levels, glw, 128),
            twice(levels + 1, glw, 128),
            twice(levels + 1, gsw, 128),
            twice(levels, gsw, 128),
            twice(glw + gsw, 256),
            pltpu.VMEM((glw, 128), F32),
            pltpu.VMEM((gsw, 128), F32),
            pltpu.VMEM((gsw, 128), F32),
            pltpu.VMEM((levels + 1, 8, columns), F32),
            pltpu.VMEM((levels + 1, 8, columns), F32),
            pltpu.SemaphoreType.DMA((2,)),
        ],
        compiler_params=pltpu.CompilerParams(vmem_limit_bytes=60 * MIB),
        cost_estimate=pl.CostEstimate(flops=250 * count, bytes_accessed=12 * MIB, transcendentals=4 * count),
        name="flux",
    )(recv, fields_base, kept, coefficients, weights, coszen, albedo, ground, sunlit)


def local_kernel(me_ref, map_ref, heat_ref, out_ref):
    columns = map_ref.shape[1]
    goal = lax.broadcasted_iota(jnp.int32, (columns, columns), 0) + me_ref[0] * columns
    stay = onehot(map_ref[...] == goal)
    high, low = halves(heat_ref[...])
    out_ref[...] = jnp.dot(high, stay, preferred_element_type=F32) + jnp.dot(
        low, stay, preferred_element_type=F32
    )


def unpack_kernel(local_ref, pick_ref, back_ref, out_ref):
    devices = back_ref.shape[0] // 2
    levels = local_ref.shape[0]
    total = local_ref[...]
    for pair in range(2):
        high, low = halves(back_ref[pl.ds(pair, devices, stride=2), :])
        for side in range(2):
            place = 2 * pair + side
            pick = pick_ref[place * devices : (place + 1) * devices, :]
            part = lax.dot_general(high, pick, TN, preferred_element_type=F32) + lax.dot_general(
                low, pick, TN, preferred_element_type=F32
            )
            total = total + part[side * levels : (side + 1) * levels]
    out_ref[...] = total


def shards(
    dyn_state,
    span_map,
    sunlit,
    coszen,
    albedo,
    ground_temp,
    aerosol,
    k_long,
    planck,
    k_short,
    solar_flux,
):
    fields, levels, columns = dyn_state.shape
    devices = lax.axis_size("gx") * lax.axis_size("gy")
    me = lax.axis_index(AXES).astype(jnp.int32).reshape(1)
    map_row = span_map.reshape(1, columns)
    swap = functools.partial(lax.all_to_all, axis_name=AXES, split_axis=0, concat_axis=0, tiled=True)

    outgoing, pick = pack(me, map_row, dyn_state, devices)
    width = outgoing.shape[1]
    recv = swap(outgoing.reshape(devices, 2 * CAP, width)).reshape(devices * 2 * CAP, width)
    fields_base, kept, coefficients, weights = base(
        me, map_row, dyn_state, aerosol, k_long, k_short, planck, solar_flux
    )
    row = lambda x: x.reshape(1, columns)
    heat, surface, back = flux(
        recv,
        fields_base,
        kept,
        coefficients,
        weights,
        row(coszen),
        row(albedo),
        row(ground_temp),
        row(sunlit),
        fields,
        planck.shape[0],
    )

    returned = swap(back.reshape(devices, 2, 128)).reshape(devices * 2, 128)
    whole = pl.BlockSpec(memory_space=pltpu.VMEM)
    local = pl.pallas_call(
        local_kernel,
        in_specs=[pl.BlockSpec(memory_space=pltpu.SMEM), whole, whole],
        out_specs=whole,
        out_shape=jax.ShapeDtypeStruct((levels, columns), F32),
        cost_estimate=pl.CostEstimate(
            flops=4 * levels * columns * columns, bytes_accessed=MIB, transcendentals=0
        ),
        name="local",
    )(me, map_row, heat)
    heating = pl.pallas_call(
        unpack_kernel,
        in_specs=[whole] * 3,
        out_specs=whole,
        out_shape=jax.ShapeDtypeStruct((levels, columns), F32),
        cost_estimate=pl.CostEstimate(
            flops=8 * levels * columns * columns, bytes_accessed=MIB, transcendentals=0
        ),
        name="unpack",
    )(local, pick, returned)
    return heating, surface


def solution(mesh):
    cols = P(AXES)
    in_specs = (
        P(None, None, AXES),
        cols,
        cols,
        cols,
        cols,
        cols,
        P(None, None, AXES),
        P(),
        P(),
        P(),
        P(),
    )
    out_specs = (P(None, AXES), P(None, AXES))
    return jax.shard_map(shards, mesh=mesh, in_specs=in_specs, out_specs=out_specs, check_vma=False)
```

time: 137 us -> 115 us (0.84)
  Pallas kernels: 78 us -> 59.2 us
  local copies, waits for them, and re-layouts: 5.7 us -> 3.74 us
    pallas_call x1, Pallas kernels: 56.6 us -> 35 us  [flux(): pl.pallas_call(flux_kernel, in_specs=[pl.BlockSpec(memory_space=pl.ANY)]...]
    pallas_call x1, Pallas kernels: 7.57 us -> 10.1 us  [pack(): pl.pallas_call(pack_kernel, grid=(steps + 1,), in_specs=[pl.BlockSpec(mem...]
    broadcast_in_dim x4 -> x0, local copies, waits for them, and re-layouts: 1.4 us -> none  [the longest x2 1.39 us: shards(): wide = lambda x: jnp.broadcast_to(x[:, None], (x.shape[0], 128))]
    unnamed x30 -> x10, local copies, waits for them, and re-layouts: 4.14 us -> 3.74 us
  transfers between devices with their start and end apart: 2 -> 2, of which waited for: 2 -> 2; matrix products, arithmetic and copies ran while one was open for 1% -> 1% of each run, Pallas kernels for 8% -> 10%
where the time goes in v1:
time: 115 us
  Pallas kernels  59.2 us (51%)
  waiting for transfers between devices  34.8 us (30%)
  starting transfers between devices  16.3 us (14%)
  local copies, waits for them, and re-layouts  3.74 us (3%)
    pallas_call x1, Pallas kernels, flux(): pl.pallas_call(flux_kernel, in_specs=[pl.BlockSpec(memory_space=pl.ANY)]...  35 us
    all_to_all x1, waiting for transfers between devices, shards(): swap(outgoing.reshape(devices, 2 * CAP, width))  26.6 us
    all_to_all x1, starting transfers between devices, shards(): swap(outgoing.reshape(devices, 2 * CAP, width))  11.5 us
    pallas_call x1, Pallas kernels, pack(): pl.pallas_call(pack_kernel, grid=(steps + 1,), in_specs=[pl.BlockSpec(mem...  10.1 us
    pallas_call x1, Pallas kernels, base(): pl.pallas_call(base_kernel, grid=(levels // depth,), in_specs=[pl.BlockSp...  10.1 us
    all_to_all x1, waiting for transfers between devices, shards(): returned = swap(back.reshape(devices, 2, 128)).reshape(devices * 2, 128)  8.16 us
    all_to_all x1, starting transfers between devices, shards(): returned = swap(back.reshape(devices, 2, 128)).reshape(devices * 2, 128)  4.79 us
    unnamed x10, local copies, waits for them, and re-layouts  3.74 us
  transfers between devices with their start and end apart: 2, of which 2 were waited for; matrix products, arithmetic and copies ran while one was open for 1% of the time, Pallas kernels for 10%

profile of v1, /device:TPU:1, one launch (start us, length us, event | category | flops | bytes accessed | tf_op | source)
XLA Modules:
  0.0 114.7 jit_solution(2078206835722348106)
XLA Ops:
  0.6 10.1 %pack.1 = (bf16[1024,1408]{1,0:T(8,128)(2,1)}, bf16[512,512]{1,0:T(8,128)(2,1)}) custom-call(s32[1]{0:T(128)} %bitcast.me_ref, s32[1,512]{1,0:T(1,128)} %bitcast.16, bf16[40,64,512]{2,1,0:T(8,128)(2,1)} %dyn_ref.3), custom_call_target="tpu_custom_call" | custom-call | flops 1342177280 | bytes 6291456 | tf_op jit(solution)/shard_map/pack/pallas_call | solution.py:85
  10.7 0.0 copy-start.2
  10.7 0.0 copy-start.3
  10.7 11.5 %all-to-all-start = ((bf16[128,8,1408]{2,1,0:T(8,128)(2,1)}), bf16[128,8,1408]{2,1,0:T(8,128)(2,1)S(1)}, u32[]{:S(2)}, u32[]{:S(2)}) async-start(bf16[128,8,1408]{2,1,0:T(8,128)(2,1)} %bitcast.13), calls=%async_computation | async-start | bytes 5767168 | tf_op jit(solution)/shard_map/all_to_all | solution.py:529
  22.2 0.0 copy-done.2
  22.2 0.7 copy.14.short_ref
  23.0 0.0 copy-done.3
  23.0 0.7 copy.13.long_ref
  23.7 10.1 %base.1 = (bf16[4,64,112,128]{3,2,1,0:T(8,128)(2,1)}, f32[64,512]{1,0:T(8,128)}, bf16[240,160]{1,0:T(8,128)(2,1)}, f32[240,128]{1,0:T(8,128)}) custom-call(s32[1]{0:T(128)} %bitcast.me_ref, s32[1,512]{1,0:T(1,128)} %bitcast.17, bf16[40,64,512]{2,1,0:T(8,128)(2,1)} %dyn_ref.3, bf16[58,64,512]{2,1,0:T(8,128)(2,1)} %aer_ref.1, bf16[128,98]{1,0:T(8,128)(2,1)} %copy.13.long_ref, ...), custom_call_target="tpu_custom_call" | custom-call | flops 1342177280 | bytes 14680064 | tf_op jit(solution)/shard_map/base/pallas_call | solution.py:184
  33.8 26.6 %all-to-all-done = bf16[128,8,1408]{2,1,0:T(8,128)(2,1)S(1)} async-done(((bf16[128,8,1408]{2,1,0:T(8,128)(2,1)}), bf16[128,8,1408]{2,1,0:T(8,128)(2,1)S(1)}, u32[]{:S(2)}, u32[]{:S(2)}) %all-to-all-start) | async-done | bytes 2883616 | tf_op jit(solution)/shard_map/all_to_all | solution.py:529
  60.4 0.0 copy-start
  60.4 1.6 %copy-done = bf16[128,8,1408]{2,1,0:T(8,128)(2,1)} copy-done((bf16[128,8,1408]{2,1,0:T(8,128)(2,1)}, bf16[128,8,1408]{2,1,0:T(8,128)(2,1)S(1)}, u32[]{:S(2)}) %copy-start) | copy-done | bytes 2883608
  62.0 35.0 %flux.1 = (f32[64,512]{1,0:T(8,128)}, f32[2,512]{1,0:T(2,128)}, f32[256,128]{1,0:T(8,128)}) custom-call(bf16[1024,1408]{1,0:T(8,128)(2,1)} %bitcast.12, bf16[4,64,112,128]{3,2,1,0:T(8,128)(2,1)} %get-tuple-element.12.base_hbm, f32[64,512]{1,0:T(8,128)} %get-tuple-element.13.kept_ref, bf16[240,160]{1,0:T(8,128)(2,1)} %get-tuple-element.14.k_ref, ...), custom_call_target="tpu_custom_call" | custom-call | flops 1966080000 | bytes 12582912 | tf_op jit(solution)/shard_map/flux/pallas_call | solution.py:449
  97.0 4.8 %all-to-all-start.1 = ((f32[128,2,128]{2,1,0:T(2,128)}), f32[128,2,128]{2,1,0:T(2,128)S(1)}, u32[]{:S(2)}, u32[]{:S(2)}) async-start(f32[128,2,128]{2,1,0:T(2,128)} %bitcast.15), calls=%async_computation.1 | async-start | bytes 262144 | tf_op jit(solution)/shard_map/all_to_all | solution.py:548
  101.8 1.9 %local.1.local_ref = f32[64,512]{1,0:T(8,128)} custom-call(s32[1]{0:T(128)} %bitcast.me_ref, s32[1,512]{1,0:T(1,128)} %bitcast.18, f32[64,512]{1,0:T(8,128)} %get-tuple-element.16.heat_ref), custom_call_target="tpu_custom_call" | custom-call | flops 67108864 | bytes 1048576 | tf_op jit(solution)/shard_map/local/pallas_call | solution.py:550
  103.7 8.2 %all-to-all-done.1 = f32[128,2,128]{2,1,0:T(2,128)S(1)} async-done(((f32[128,2,128]{2,1,0:T(2,128)}), f32[128,2,128]{2,1,0:T(2,128)S(1)}, u32[]{:S(2)}, u32[]{:S(2)}) %all-to-all-start.1) | async-done | bytes 131104 | tf_op jit(solution)/shard_map/all_to_all | solution.py:548
  111.8 0.0 copy-start.1
  111.8 0.7 copy-done.1
  112.5 2.2 %unpack.1 = f32[64,512]{1,0:T(8,128)} custom-call(f32[64,512]{1,0:T(8,128)} %local.1.local_ref, bf16[512,512]{1,0:T(8,128)(2,1)} %get-tuple-element.17.pick_ref, f32[256,128]{1,0:T(8,128)} %bitcast.14), custom_call_target="tpu_custom_call" | custom-call | flops 134217728 | bytes 1048576 | tf_op jit(solution)/shard_map/unpack/pallas_call | solution.py:560
Async XLA Ops:
  10.7 11.5 %copy-start.2 = (bf16[112,98]{0,1:T(8,128)(2,1)S(1)}, bf16[112,98]{0,1:T(8,128)(2,1)}, u32[]{:S(2)}) copy-start(bf16[112,98]{0,1:T(8,128)(2,1)} %param.20) | copy-start | bytes 65860
  10.7 12.2 %copy-start.3 = (bf16[128,98]{0,1:T(8,128)(2,1)S(1)}, bf16[128,98]{0,1:T(8,128)(2,1)}, u32[]{:S(2)}) copy-start(bf16[128,98]{0,1:T(8,128)(2,1)} %param.18) | copy-start | bytes 75268
  10.7 49.6 %all-to-all-start = ((bf16[128,8,1408]{2,1,0:T(8,128)(2,1)}), bf16[128,8,1408]{2,1,0:T(8,128)(2,1)S(1)}, u32[]{:S(2)}, u32[]{:S(2)}) async-start(bf16[128,8,1408]{2,1,0:T(8,128)(2,1)} %bitcast.13), calls=%async_computation | async-start | bytes 5767168 | tf_op jit(solution)/shard_map/all_to_all | solution.py:529
  60.4 1.6 %copy-start = (bf16[128,8,1408]{2,1,0:T(8,128)(2,1)}, bf16[128,8,1408]{2,1,0:T(8,128)(2,1)S(1)}, u32[]{:S(2)}) copy-start(bf16[128,8,1408]{2,1,0:T(8,128)(2,1)S(1)} %all-to-all-done) | copy-start | bytes 8650756
  97.0 14.8 %all-to-all-start.1 = ((f32[128,2,128]{2,1,0:T(2,128)}), f32[128,2,128]{2,1,0:T(2,128)S(1)}, u32[]{:S(2)}, u32[]{:S(2)}) async-start(f32[128,2,128]{2,1,0:T(2,128)} %bitcast.15), calls=%async_computation.1 | async-start | bytes 262144 | tf_op jit(solution)/shard_map/all_to_all | solution.py:548
  111.8 0.7 copy-start.1

commit v2 on v1

v2 whole, which is shorter than its diff:
```python
import functools

import jax
import jax.numpy as jnp
from jax import lax
from jax.experimental import pallas as pl
from jax.experimental.pallas import tpu as pltpu
from jax.sharding import PartitionSpec as P

AXES = ("gx", "gy")
DIFFUSE = 1.66
SCATTER = 0.3
SW_DEPTH = 2.0
LOG2E = 1.4426950408889634
CAP = 4
BF16 = jnp.bfloat16
F32 = jnp.float32
NT = (((1,), (1,)), ((), ()))
TN = (((0,), (0,)), ((), ()))
MIB = 1 << 20
HEAD, TAIL = 48, 64


def onehot(mask):
    return jnp.where(mask, 1.0, 0.0).astype(BF16)


def halves(x):
    high = x.astype(BF16)
    return high, (x - high.astype(F32)).astype(BF16)


def softplus2(u):
    return jnp.maximum(u, jnp.log2(1.0 + jnp.exp2(jnp.minimum(u, 126.0))))


def pack_kernel(me_ref, map_ref, dyn_ref, out_ref, pick_ref, place_ref, meta_ref):
    columns = map_ref.shape[1]
    rows = place_ref.shape[0]
    devices = rows // (2 * CAP)
    step = pl.program_id(0)
    last = pl.num_programs(0) - 1

    @pl.when(step == 0)
    def _():
        where_to = map_ref[...]
        target = where_to // columns
        slot = where_to % columns
        same = target == lax.broadcasted_iota(jnp.int32, (devices, columns), 0)
        earlier = onehot(
            lax.broadcasted_iota(jnp.int32, (columns, columns), 0)
            < lax.broadcasted_iota(jnp.int32, (columns, columns), 1)
        )
        before = jnp.dot(onehot(same), earlier, preferred_element_type=F32)
        rank = jnp.sum(jnp.where(same, before, 0.0), axis=0, keepdims=True).astype(jnp.int32)
        rank = jnp.where(target == me_ref[0], CAP, rank)
        for place in range(CAP):
            pick_ref[place * devices : (place + 1) * devices, :] = onehot(same & (rank == place))
        key = jnp.where(rank < CAP, (target * CAP + rank) * 2, 2 * rows)
        line = lax.broadcasted_iota(jnp.int32, (128, columns), 0)
        mark = slot + 1
        meta = jnp.where(line == 0, mark // 2, jnp.where(line == 1, mark % 2, 0)).astype(F32)
        for half in range(2):
            lanes = slice(half * columns, (half + 1) * columns)
            meta_ref[:, lanes] = meta.astype(BF16)
            for start in range(0, rows, 128):
                line = lax.broadcasted_iota(jnp.int32, (128, columns), 0) + start
                place_ref[start : start + 128, lanes] = onehot(line == key + half)

    @pl.when(step < last)
    def _():
        count = dyn_ref.shape[0] * 32
        both = [dyn_ref[:, half * 32 : half * 32 + 32, :].reshape(count, columns) for half in range(2)]
        out_ref[...] = lax.dot_general(
            place_ref[...], jnp.concatenate(both, axis=1), NT, preferred_element_type=F32
        ).astype(BF16)

    @pl.when(step == last)
    def _():
        out_ref[:, :128] = lax.dot_general(
            place_ref[...], meta_ref[...], NT, preferred_element_type=F32
        ).astype(BF16)


def pack(me, map_row, dyn_state, devices):
    fields, levels, columns = dyn_state.shape
    steps = fields // 8
    rows = devices * CAP * 2
    return pl.pallas_call(
        pack_kernel,
        grid=(steps + 1,),
        in_specs=[
            pl.BlockSpec(memory_space=pltpu.SMEM),
            pl.BlockSpec((1, columns), lambda i: (0, 0)),
            pl.BlockSpec((8, levels, columns), lambda i: (jnp.minimum(i, steps - 1), 0, 0)),
        ],
        out_specs=[
            pl.BlockSpec((rows, 256), lambda i: (0, i)),
            pl.BlockSpec((devices * CAP, columns), lambda i: (0, 0)),
        ],
        out_shape=[
            jax.ShapeDtypeStruct((rows, steps * 256 + 128), BF16),
            jax.ShapeDtypeStruct((devices * CAP, columns), BF16),
        ],
        scratch_shapes=[
            pltpu.VMEM((rows, 2 * columns), BF16),
            pltpu.VMEM((128, 2 * columns), BF16),
        ],
        compiler_params=pltpu.CompilerParams(vmem_limit_bytes=56 * MIB),
        cost_estimate=pl.CostEstimate(
            flops=4 * fields * levels * columns * devices * CAP, bytes_accessed=6 * MIB, transcendentals=0
        ),
        name="pack",
    )(me, map_row, dyn_state)


def base_kernel(
    me_ref,
    map_ref,
    dyn_ref,
    aer_ref,
    long_ref,
    short_ref,
    planck_ref,
    solar_ref,
    aero_ref,
    kept_ref,
    k_ref,
    weight_ref,
    pick_ref,
    rows_ref,
    wide_ref,
):
    fields, depth, columns = dyn_ref.shape
    extra = aer_ref.shape[0]
    tiles = columns // 128
    glw, gsw = long_ref.shape[0], short_ref.shape[0]

    @pl.when(pl.program_id(0) == 0)
    def _():
        goal = lax.broadcasted_iota(jnp.int32, (columns, columns), 0) + me_ref[0] * columns
        pick_ref[...] = onehot(map_ref[...] == goal)
        wide_ref[...] = jnp.zeros(wide_ref.shape, F32)
        for coefficients, start in ((long_ref[...], 0), (short_ref[...], glw)):
            scaled = coefficients.astype(F32) * LOG2E
            rows = slice(start, start + coefficients.shape[0])
            for first, part in zip((0, HEAD + TAIL), halves(scaled)):
                part = part.astype(F32)
                wide_ref[rows, first : first + fields] = part[:, :fields]
                wide_ref[rows, first + HEAD : first + HEAD + extra] = part[:, fields:]
        k_ref[...] = wide_ref[...].astype(BF16)
        square = lax.broadcasted_iota(jnp.int32, (128, 128), 0) == lax.broadcasted_iota(
            jnp.int32, (128, 128), 1
        )
        for source, start in ((planck_ref[...], 0), (solar_ref[...], glw)):
            size = source.shape[1]
            picked = jnp.where(square[:size, :size], source, 0.0)
            weight_ref[start : start + size, :] = jnp.broadcast_to(
                jnp.sum(picked, axis=1, keepdims=True), (size, 128)
            )

    kept = lax.dot_general(
        dyn_ref[...].reshape(fields * depth, columns), pick_ref[...], NT, preferred_element_type=F32
    )
    kept_ref[0] = kept.astype(BF16).reshape(fields, depth, columns)
    more = aer_ref[...].reshape(extra * depth, columns).astype(F32)
    for tile in range(tiles):
        rows_ref[tile] = more[:, tile * 128 : tile * 128 + 128]
    for tile in range(tiles):
        for level in range(depth):
            aero = rows_ref[tile, pl.ds(level, extra, stride=depth), :]
            aero_ref[tile, level] = jnp.concatenate(
                [aero, jnp.zeros((TAIL - extra, 128), F32)], axis=0
            ).astype(BF16)


def base(me, map_row, dyn_state, aerosol, k_long, k_short, planck, solar):
    fields, levels, columns = dyn_state.shape
    extra = aerosol.shape[0]
    glw, gsw = k_long.shape[0], k_short.shape[0]
    depth = 16
    tiles = columns // 128
    fixed = lambda *shape: pl.BlockSpec(shape, lambda i: (0,) * len(shape))
    return pl.pallas_call(
        base_kernel,
        grid=(levels // depth,),
        in_specs=[
            pl.BlockSpec(memory_space=pltpu.SMEM),
            fixed(1, columns),
            pl.BlockSpec((fields, depth, columns), lambda i: (0, i, 0)),
            pl.BlockSpec((extra, depth, columns), lambda i: (0, i, 0)),
            fixed(*k_long.shape),
            fixed(*k_short.shape),
            fixed(1, glw),
            fixed(1, gsw),
        ],
        out_specs=[
            pl.BlockSpec((tiles, depth, TAIL, 128), lambda i: (0, i, 0, 0)),
            pl.BlockSpec((1, fields, depth, columns), lambda i: (i // 2, 0, i % 2, 0)),
            fixed(glw + gsw, 2 * (HEAD + TAIL)),
            fixed(glw + gsw, 128),
        ],
        out_shape=[
            jax.ShapeDtypeStruct((tiles, levels, TAIL, 128), BF16),
            jax.ShapeDtypeStruct((2, fields, levels // 2, columns), BF16),
            jax.ShapeDtypeStruct((glw + gsw, 2 * (HEAD + TAIL)), BF16),
            jax.ShapeDtypeStruct((glw + gsw, 128), F32),
        ],
        scratch_shapes=[
            pltpu.VMEM((columns, columns), BF16),
            pltpu.VMEM((tiles, extra * depth, 128), F32),
            pltpu.VMEM((glw + gsw, 2 * (HEAD + TAIL)), F32),
        ],
        compiler_params=pltpu.CompilerParams(vmem_limit_bytes=56 * MIB),
        cost_estimate=pl.CostEstimate(
            flops=2 * fields * levels * columns * columns, bytes_accessed=14 * MIB, transcendentals=0
        ),
        name="base",
    )(me, map_row, dyn_state, aerosol, k_long, k_short, planck.reshape(1, glw), solar.reshape(1, gsw))


def flux_kernel(
    recv_hbm,
    aero_hbm,
    kept_hbm,
    k_ref,
    weight_ref,
    cos_ref,
    albedo_ref,
    ground_ref,
    lit_ref,
    heat_ref,
    surface_ref,
    back_ref,
    recv_ref,
    aero_ref,
    kept_ref,
    pick_ref,
    state_ref,
    delta_ref,
    trans_refs,
    down_refs,
    scat_refs,
    diff_refs,
    depth_refs,
    up_ref,
    beam_ref,
    spread_ref,
    return_ref,
    net_lw_ref,
    net_sw_ref,
    sems,
):
    rows = recv_ref.shape[0]
    devices = rows // (2 * CAP)
    tiles, levels, _, _ = aero_ref.shape
    columns = 128 * tiles
    glw, gsw = up_ref.shape[0], return_ref.shape[0]
    tall = state_ref.shape[1]
    fields = tall // 32
    pairs = levels // 2

    copies = [
        pltpu.make_async_copy(source, target, sems.at[i])
        for i, (source, target) in enumerate(
            [(recv_hbm, recv_ref), (kept_hbm, kept_ref)]
            + [(aero_hbm.at[tile], aero_ref.at[tile]) for tile in range(tiles)]
        )
    ]
    for copy in copies:
        copy.start()

    lanes_of = lambda tile: slice(tile * 128, tile * 128 + 128)
    copies[0].wait()
    mark = recv_ref[:, tall : tall + 128].astype(F32)
    mark = (mark[:, 0:1] * 2.0 + mark[:, 1:2]).astype(jnp.int32)
    half_of = lax.broadcasted_iota(jnp.int32, (rows, 1), 0) % 2
    for half in range(2):
        key = jnp.where(half_of == half, mark, 0)
        for tile in range(0, columns, 128):
            lane = lax.broadcasted_iota(jnp.int32, (rows, 128), 1) + (tile + 1)
            pick_ref[:, half * columns + tile : half * columns + tile + 128] = onehot(key == lane)
    copies[1].wait()
    for tile in range(0, tall, 128):
        moved = lax.dot_general(
            recv_ref[:, tile : tile + 128], pick_ref[...], TN, preferred_element_type=F32
        )
        for part in range(2 * tiles):
            stayed = kept_ref[part // tiles, tile // 32 : tile // 32 + 4, :, lanes_of(part % tiles)]
            state_ref[part, tile : tile + 128, :] = moved[:, lanes_of(part)] + stayed.reshape(
                128, 128
            ).astype(F32)

    for tile in range(tiles):
        cold = jnp.concatenate([state_ref[tile, :32, :], state_ref[tiles + tile, :32, :]], axis=0)
        warmth = softplus2(cold * LOG2E) * (1.0 / LOG2E)
        step = warmth - jnp.concatenate([warmth[1:], jnp.zeros((1, 128), F32)], axis=0)
        delta_ref[0, :, lanes_of(tile)] = jnp.broadcast_to(warmth[0:1], (8, 128))
        for level in range(levels):
            delta_ref[level + 1, :, lanes_of(tile)] = jnp.broadcast_to(step[level : level + 1], (8, 128))

    cosine, albedo, ground = cos_ref[...], albedo_ref[...], ground_ref[...]
    lit = lit_ref[...].astype(F32)
    slant = (-SW_DEPTH / levels) / cosine
    skin = softplus2(ground * LOG2E) * (1.0 / LOG2E)

    def absorb(pair, tile):
        half = pair // (pairs // 2)
        inner = 2 * pair - 32 * half
        both = [
            state_ref[half * tiles + tile, pl.ds(inner + e, fields, stride=32), :] for e in range(2)
        ]
        here = jnp.concatenate(
            [jnp.concatenate(both, axis=1), jnp.zeros((HEAD - fields, 256), F32)], axis=0
        ).astype(BF16)
        rest = jnp.concatenate([aero_ref[tile, 2 * pair + e] for e in range(2)], axis=1)
        return jnp.dot(
            k_ref[...], jnp.concatenate([here, rest, here, rest], axis=0), preferred_element_type=F32
        )

    def both_ways(pair, tile, depth_ref, following, following_tile, following_ref):
        descends, ascends = tile < tiles, tile > 0
        if descends:
            following_ref[...] = absorb(following, following_tile)
            trans_ref, down_ref = trans_refs[tile % 2], down_refs[tile % 2]
            scat_ref, diff_ref = scat_refs[tile % 2], diff_refs[tile % 2]
            level = 2 * pair
            lanes = lanes_of(tile)
            delta = [delta_ref[level + e + 1, :, lanes] for e in range(2)]
            slope = jnp.broadcast_to(slant[:, lanes], (8, 128))
            sum_beam = [jnp.zeros((8, 128), F32) for _ in range(2)]
            sum_spread = [jnp.zeros((8, 128), F32) for _ in range(2)]
        if ascends:
            old_trans, old_down = trans_refs[1 - tile % 2], down_refs[1 - tile % 2]
            old_scat, old_diff = scat_refs[1 - tile % 2], diff_refs[1 - tile % 2]
            old_level = 2 * (pairs - 1 - pair)
            old_lanes = lanes_of(tile - 1)
            old_delta = [delta_ref[old_level + e, :, old_lanes] for e in range(2)]
            total_lw = [jnp.zeros((8, 128), F32) for _ in range(2)]
            total_sw = [net_sw_ref[old_level + e, :, old_lanes] for e in range(2)]

        for g in range(0, glw, 8):
            if descends:
                down = down_ref[level, g : g + 8, :]
                for e in range(2):
                    u = depth_ref[g : g + 8, 128 * e : 128 * e + 128]
                    tau = jnp.log2(1.0 + jnp.exp2(jnp.minimum(u, 126.0)))
                    trans = jnp.exp2(tau * (-DIFFUSE))
                    trans_ref[level + e, g : g + 8, :] = trans
                    down = trans * down + delta[e]
                    down_ref[level + e + 1, g : g + 8, :] = down
            if ascends:
                upper = up_ref[g : g + 8, :]
                weight = weight_ref[g : g + 8, :]
                for e in (1, 0):
                    passed = old_trans[old_level + e, g : g + 8, :] * upper
                    total_lw[e] = total_lw[e] + weight * (old_down[old_level + e, g : g + 8, :] - passed)
                    upper = passed - old_delta[e]
                up_ref[g : g + 8, :] = upper
        for g in range(0, gsw, 8):
            if descends:
                beam = beam_ref[g : g + 8, :]
                spread = spread_ref[g : g + 8, :]
                for e in range(2):
                    u = depth_ref[glw + g : glw + g + 8, 128 * e : 128 * e + 128]
                    tau = jnp.maximum(u, jnp.log2(1.0 + jnp.exp2(jnp.minimum(u, 126.0))))
                    diffuse = jnp.exp2(tau * (-DIFFUSE * SW_DEPTH / levels))
                    diff_ref[level + e, g : g + 8, :] = diffuse
                    lower = jnp.exp2(tau * slope) * beam
                    scattered = beam - lower
                    scat_ref[level + e, g : g + 8, :] = scattered
                    sum_beam[e] = sum_beam[e] + beam
                    sum_spread[e] = sum_spread[e] + spread
                    spread = diffuse * spread + scattered
                    beam = lower
                beam_ref[g : g + 8, :] = beam
                spread_ref[g : g + 8, :] = spread
            if ascends:
                upper = return_ref[g : g + 8, :]
                for e in (1, 0):
                    upper = (
                        old_diff[old_level + e, g : g + 8, :] * upper
                        + old_scat[old_level + e, g : g + 8, :]
                    )
                    total_sw[e] = total_sw[e] - upper
                return_ref[g : g + 8, :] = upper
        for e in range(2):
            if descends:
                net_sw_ref[level + e, :, lanes] = sum_beam[e] * (1.0 / SCATTER) + sum_spread[e]
            if ascends:
                net_lw_ref[old_level + e, :, old_lanes] = total_lw[e]
                net_sw_ref[old_level + e, :, old_lanes] = total_sw[e]

    def turn(tile):
        lanes = lanes_of(tile)
        down_ref = down_refs[tile % 2]
        total = jnp.zeros((8, 128), F32)
        floor_total = jnp.zeros((8, 128), F32)
        upper = jnp.broadcast_to(skin[:, lanes], (8, 128))
        above = upper - delta_ref[levels, :, lanes]
        for g in range(0, glw, 8):
            weight = weight_ref[g : g + 8, :]
            floor = weight * down_ref[levels, g : g + 8, :]
            floor_total = floor_total + floor
            total = total + (floor - weight * upper)
            up_ref[g : g + 8, :] = above
        net_lw_ref[levels, :, lanes] = total
        surface_ref[0:1, lanes] = jnp.sum(floor_total, axis=0, keepdims=True) * (1.0 / glw)
        bright = jnp.broadcast_to(albedo[:, lanes], (8, 128))
        floor_total = jnp.zeros((8, 128), F32)
        for g in range(0, gsw, 8):
            floor = beam_ref[g : g + 8, :] * (1.0 / SCATTER) + spread_ref[g : g + 8, :]
            floor_total = floor_total + floor
            return_ref[g : g + 8, :] = bright * floor
        net_sw_ref[levels, :, lanes] = floor_total - bright * floor_total
        surface_ref[1:2, lanes] = jnp.sum(floor_total, axis=0, keepdims=True) * (
            lit[:, lanes] * cosine[:, lanes] * (1.0 / gsw)
        )

    copies[2].wait()
    depth_refs[0][...] = absorb(0, 0)
    for tile in range(tiles + 1):
        if tile + 1 < tiles:
            copies[2 + tile + 1].wait()
        if tile < tiles:
            first = 0.0 - delta_ref[0, :, lanes_of(tile)]
            for g in range(0, glw, 8):
                down_refs[tile % 2][0, g : g + 8, :] = first
            spread_ref[...] = jnp.zeros((gsw, 128), F32)
            beam_ref[...] = SCATTER * weight_ref[glw:, :]

        def two_pairs(step, _, tile=tile):
            for part in range(2):
                pair = 2 * step + part
                over = pair == pairs - 1
                following = jnp.where(over, 0, pair + 1)
                following_tile = jnp.where(over, min(tile + 1, tiles - 1), tile)
                both_ways(
                    pair, tile, depth_refs[part], following, following_tile, depth_refs[1 - part]
                )
            return 0

        lax.fori_loop(0, pairs // 2, two_pairs, 0, unroll=4)
        if tile < tiles:
            turn(tile)

    net_lw = jnp.sum(net_lw_ref[...], axis=1)
    net_sw = jnp.sum(net_sw_ref[...], axis=1)
    heat = (net_lw[:levels] - net_lw[1 : levels + 1]) * (1.0 / glw) + (
        net_sw[:levels] - net_sw[1 : levels + 1]
    ) * (lit * cosine * (1.0 / gsw))
    heat_ref[...] = heat

    twice = jnp.concatenate([heat, heat], axis=0)
    high, low = halves(twice)
    picked = pick_ref[:, :columns]
    state_ref[0, :rows, :] = lax.dot_general(picked, high, NT, preferred_element_type=F32) + lax.dot_general(
        picked, low, NT, preferred_element_type=F32
    )
    left = lax.broadcasted_iota(jnp.int32, (devices, 128), 1) < levels
    for pair in range(2):
        even = state_ref[0, pl.ds(4 * pair, devices, stride=8), :]
        odd = state_ref[0, pl.ds(4 * pair + 2, devices, stride=8), :]
        back_ref[pl.ds(pair, devices, stride=2), :] = jnp.where(left, even, odd)


def flux(recv, aero, kept, coefficients, weights, coszen, albedo, ground, sunlit, fields, glw):
    rows, width = recv.shape
    tiles, levels, _, _ = aero.shape
    columns = 128 * tiles
    gsw = weights.shape[0] - glw
    devices = rows // (2 * CAP)
    whole = pl.BlockSpec(memory_space=pltpu.VMEM)
    count = (glw + gsw) * levels * columns
    twice = lambda *shape: [pltpu.VMEM(shape, F32)] * 2
    return pl.pallas_call(
        flux_kernel,
        in_specs=[pl.BlockSpec(memory_space=pl.ANY)] * 3 + [whole] * 6,
        out_specs=[whole] * 3,
        out_shape=[
            jax.ShapeDtypeStruct((levels, columns), F32),
            jax.ShapeDtypeStruct((2, columns), F32),
            jax.ShapeDtypeStruct((devices * 2, 128), F32),
        ],
        scratch_shapes=[
            pltpu.VMEM((rows, width), BF16),
            pltpu.VMEM(aero.shape, BF16),
            pltpu.VMEM(kept.shape, BF16),
            pltpu.VMEM((rows, 2 * columns), BF16),
            pltpu.VMEM((2 * tiles, fields * 32, 128), F32),
            pltpu.VMEM((levels + 1, 8, columns), F32),
            twice(levels, glw, 128),
            twice(levels + 1, glw, 128),
            twice(levels, gsw, 128),
            twice(levels, gsw, 128),
            twice(glw + gsw, 256),
            pltpu.VMEM((glw, 128), F32),
            pltpu.VMEM((gsw, 128), F32),
            pltpu.VMEM((gsw, 128), F32),
            pltpu.VMEM((gsw, 128), F32),
            pltpu.VMEM((levels + 1, 8, columns), F32),
            pltpu.VMEM((levels + 1, 8, columns), F32),
            pltpu.SemaphoreType.DMA((2 + tiles,)),
        ],
        compiler_params=pltpu.CompilerParams(vmem_limit_bytes=54 * MIB),
        cost_estimate=pl.CostEstimate(flops=250 * count, bytes_accessed=12 * MIB, transcendentals=4 * count),
        name="flux",
    )(recv, aero, kept, coefficients, weights, coszen, albedo, ground, sunlit)


def local_kernel(me_ref, map_ref, heat_ref, out_ref):
    columns = map_ref.shape[1]
    goal = lax.broadcasted_iota(jnp.int32, (columns, columns), 0) + me_ref[0] * columns
    stay = onehot(map_ref[...] == goal)
    high, low = halves(heat_ref[...])
    out_ref[...] = jnp.dot(high, stay, preferred_element_type=F32) + jnp.dot(
        low, stay, preferred_element_type=F32
    )


def unpack_kernel(local_ref, pick_ref, back_ref, out_ref):
    devices = back_ref.shape[0] // 2
    levels = local_ref.shape[0]
    total = local_ref[...]
    for pair in range(2):
        high, low = halves(back_ref[pl.ds(pair, devices, stride=2), :])
        for side in range(2):
            place = 2 * pair + side
            pick = pick_ref[place * devices : (place + 1) * devices, :]
            part = lax.dot_general(high, pick, TN, preferred_element_type=F32) + lax.dot_general(
                low, pick, TN, preferred_element_type=F32
            )
            total = total + part[side * levels : (side + 1) * levels]
    out_ref[...] = total


def shards(
    dyn_state,
    span_map,
    sunlit,
    coszen,
    albedo,
    ground_temp,
    aerosol,
    k_long,
    planck,
    k_short,
    solar_flux,
):
    fields, levels, columns = dyn_state.shape
    devices = lax.axis_size("gx") * lax.axis_size("gy")
    me = lax.axis_index(AXES).astype(jnp.int32).reshape(1)
    map_row = span_map.reshape(1, columns)
    swap = functools.partial(lax.all_to_all, axis_name=AXES, split_axis=0, concat_axis=0, tiled=True)

    outgoing, pick = pack(me, map_row, dyn_state, devices)
    width = outgoing.shape[1]
    recv = swap(outgoing.reshape(devices, 2 * CAP, width)).reshape(devices * 2 * CAP, width)
    aero, kept, coefficients, weights = base(
        me, map_row, dyn_state, aerosol, k_long, k_short, planck, solar_flux
    )
    row = lambda x: x.reshape(1, columns)
    heat, surface, back = flux(
        recv,
        aero,
        kept,
        coefficients,
        weights,
        row(coszen),
        row(albedo),
        row(ground_temp),
        row(sunlit),
        fields,
        planck.shape[0],
    )

    returned = swap(back.reshape(devices, 2, 128)).reshape(devices * 2, 128)
    whole = pl.BlockSpec(memory_space=pltpu.VMEM)
    local = pl.pallas_call(
        local_kernel,
        in_specs=[pl.BlockSpec(memory_space=pltpu.SMEM), whole, whole],
        out_specs=whole,
        out_shape=jax.ShapeDtypeStruct((levels, columns), F32),
        cost_estimate=pl.CostEstimate(
            flops=4 * levels * columns * columns, bytes_accessed=MIB, transcendentals=0
        ),
        name="local",
    )(me, map_row, heat)
    heating = pl.pallas_call(
        unpack_kernel,
        in_specs=[whole] * 3,
        out_specs=whole,
        out_shape=jax.ShapeDtypeStruct((levels, columns), F32),
        cost_estimate=pl.CostEstimate(
            flops=8 * levels * columns * columns, bytes_accessed=MIB, transcendentals=0
        ),
        name="unpack",
    )(local, pick, returned)
    return heating, surface


def solution(mesh):
    cols = P(AXES)
    in_specs = (
        P(None, None, AXES),
        cols,
        cols,
        cols,
        cols,
        cols,
        P(None, None, AXES),
        P(),
        P(),
        P(),
        P(),
    )
    out_specs = (P(None, AXES), P(None, AXES))
    return jax.shard_map(shards, mesh=mesh, in_specs=in_specs, out_specs=out_specs, check_vma=False)
```

time: 115 us -> 111 us (0.965)
  Pallas kernels: 59.2 us -> 54 us
  waiting for transfers between devices: 34.8 us -> 36.2 us
    pallas_call x1, Pallas kernels: 35 us -> 32.9 us  [flux(): pl.pallas_call(flux_kernel, in_specs=[pl.BlockSpec(memory_space=pl.ANY)]...]
    pallas_call x1, Pallas kernels: 10.1 us -> 8.3 us  [pack(): pl.pallas_call(pack_kernel, grid=(steps + 1,), in_specs=[pl.BlockSpec(mem...]
    pallas_call x1, Pallas kernels: 10.1 us -> 8.67 us  [base(): pl.pallas_call(base_kernel, grid=(levels // depth,), in_specs=[pl.BlockSp...]
    all_to_all x1, waiting for transfers between devices: 26.6 us -> 28 us  [shards(): swap(outgoing.reshape(devices, 2 * CAP, width))]
where the time goes in v2:
time: 111 us
  Pallas kernels  54 us (49%)
  waiting for transfers between devices  36.2 us (33%)
  starting transfers between devices  16.3 us (15%)
  local copies, waits for them, and re-layouts  3.7 us (3%)
    pallas_call x1, Pallas kernels, flux(): pl.pallas_call(flux_kernel, in_specs=[pl.BlockSpec(memory_space=pl.ANY)]...  32.9 us
    all_to_all x1, waiting for transfers between devices, shards(): swap(outgoing.reshape(devices, 2 * CAP, width))  28 us
    all_to_all x1, starting transfers between devices, shards(): swap(outgoing.reshape(devices, 2 * CAP, width))  11.5 us
    pallas_call x1, Pallas kernels, base(): pl.pallas_call(base_kernel, grid=(levels // depth,), in_specs=[pl.BlockSp...  8.67 us
    pallas_call x1, Pallas kernels, pack(): pl.pallas_call(pack_kernel, grid=(steps + 1,), in_specs=[pl.BlockSpec(mem...  8.3 us
    all_to_all x1, waiting for transfers between devices, shards(): returned = swap(back.reshape(devices, 2, 128)).reshape(devices * 2, 128)  8.18 us
    all_to_all x1, starting transfers between devices, shards(): returned = swap(back.reshape(devices, 2, 128)).reshape(devices * 2, 128)  4.79 us
    unnamed x10, local copies, waits for them, and re-layouts  3.7 us
  transfers between devices with their start and end apart: 2, of which 2 were waited for; matrix products, arithmetic and copies ran while one was open for 1% of the time, Pallas kernels for 10%

profile of v2, /device:TPU:1, one launch (start us, length us, event | category | flops | bytes accessed | tf_op | source)
XLA Modules:
  0.0 110.8 jit_solution(8811423354450554175)
XLA Ops:
  0.6 8.3 %pack.1 = (bf16[1024,1408]{1,0:T(8,128)(2,1)}, bf16[512,512]{1,0:T(8,128)(2,1)}) custom-call(s32[1]{0:T(128)} %bitcast.me_ref, s32[1,512]{1,0:T(1,128)} %bitcast.16, bf16[40,64,512]{2,1,0:T(8,128)(2,1)} %dyn_ref.3), custom_call_target="tpu_custom_call" | custom-call | flops 2684354560 | bytes 6291456 | tf_op jit(solution)/shard_map/pack/pallas_call | solution.py:89
  8.9 0.0 copy-start.2
  8.9 0.0 copy-start.3
  8.9 11.5 %all-to-all-start = ((bf16[128,8,1408]{2,1,0:T(8,128)(2,1)}), bf16[128,8,1408]{2,1,0:T(8,128)(2,1)S(1)}, u32[]{:S(2)}, u32[]{:S(2)}) async-start(bf16[128,8,1408]{2,1,0:T(8,128)(2,1)} %bitcast.13), calls=%async_computation | async-start | bytes 5767168 | tf_op jit(solution)/shard_map/all_to_all | solution.py:558
  20.5 0.0 copy-done.2
  20.5 0.7 copy.14.short_ref
  21.2 0.0 copy-done.3
  21.2 0.7 copy.13.long_ref
  21.9 8.7 %base.1 = (bf16[4,64,64,128]{3,2,1,0:T(8,128)(2,1)}, bf16[2,40,32,512]{3,2,1,0:T(8,128)(2,1)}, bf16[240,224]{1,0:T(8,128)(2,1)}, f32[240,128]{1,0:T(8,128)}) custom-call(s32[1]{0:T(128)} %bitcast.me_ref, s32[1,512]{1,0:T(1,128)} %bitcast.17, bf16[40,64,512]{2,1,0:T(8,128)(2,1)} %dyn_ref.3, bf16[58,64,512]{2,1,0:T(8,128)(2,1)} %aer_ref.1, ...), custom_call_target="tpu_custom_call" | custom-call | flops 1342177280 | bytes 14680064 | tf_op jit(solution)/shard_map/base/pallas_call | solution.py:184
  30.6 28.0 %all-to-all-done = bf16[128,8,1408]{2,1,0:T(8,128)(2,1)S(1)} async-done(((bf16[128,8,1408]{2,1,0:T(8,128)(2,1)}), bf16[128,8,1408]{2,1,0:T(8,128)(2,1)S(1)}, u32[]{:S(2)}, u32[]{:S(2)}) %all-to-all-start) | async-done | bytes 2883616 | tf_op jit(solution)/shard_map/all_to_all | solution.py:558
  58.6 0.0 copy-start
  58.6 1.6 %copy-done = bf16[128,8,1408]{2,1,0:T(8,128)(2,1)} copy-done((bf16[128,8,1408]{2,1,0:T(8,128)(2,1)}, bf16[128,8,1408]{2,1,0:T(8,128)(2,1)S(1)}, u32[]{:S(2)}) %copy-start) | copy-done | bytes 2883608
  60.2 32.9 %flux.1 = (f32[64,512]{1,0:T(8,128)}, f32[2,512]{1,0:T(2,128)}, f32[256,128]{1,0:T(8,128)}) custom-call(bf16[1024,1408]{1,0:T(8,128)(2,1)} %bitcast.12, bf16[4,64,64,128]{3,2,1,0:T(8,128)(2,1)} %get-tuple-element.12.aero_hbm, bf16[2,40,32,512]{3,2,1,0:T(8,128)(2,1)} %get-tuple-element.13.kept_hbm, bf16[240,224]{1,0:T(8,128)(2,1)} %get-tuple-element.14.k_ref, ...), custom_call_target="tpu_custom_call" | custom-call | flops 1966080000 | bytes 12582912 | tf_op jit(solution)/shard_map/flux/pallas_call | solution.py:476
  93.1 4.8 %all-to-all-start.1 = ((f32[128,2,128]{2,1,0:T(2,128)}), f32[128,2,128]{2,1,0:T(2,128)S(1)}, u32[]{:S(2)}, u32[]{:S(2)}) async-start(f32[128,2,128]{2,1,0:T(2,128)} %bitcast.15), calls=%async_computation.1 | async-start | bytes 262144 | tf_op jit(solution)/shard_map/all_to_all | solution.py:577
  97.9 1.9 %local.1.local_ref = f32[64,512]{1,0:T(8,128)} custom-call(s32[1]{0:T(128)} %bitcast.me_ref, s32[1,512]{1,0:T(1,128)} %bitcast.18, f32[64,512]{1,0:T(8,128)} %get-tuple-element.16.heat_ref), custom_call_target="tpu_custom_call" | custom-call | flops 67108864 | bytes 1048576 | tf_op jit(solution)/shard_map/local/pallas_call | solution.py:579
  99.8 8.2 %all-to-all-done.1 = f32[128,2,128]{2,1,0:T(2,128)S(1)} async-done(((f32[128,2,128]{2,1,0:T(2,128)}), f32[128,2,128]{2,1,0:T(2,128)S(1)}, u32[]{:S(2)}, u32[]{:S(2)}) %all-to-all-start.1) | async-done | bytes 131104 | tf_op jit(solution)/shard_map/all_to_all | solution.py:577
  108.0 0.0 copy-start.1
  108.0 0.7 copy-done.1
  108.6 2.2 %unpack.1 = f32[64,512]{1,0:T(8,128)} custom-call(f32[64,512]{1,0:T(8,128)} %local.1.local_ref, bf16[512,512]{1,0:T(8,128)(2,1)} %get-tuple-element.17.pick_ref, f32[256,128]{1,0:T(8,128)} %bitcast.14), custom_call_target="tpu_custom_call" | custom-call | flops 134217728 | bytes 1048576 | tf_op jit(solution)/shard_map/unpack/pallas_call | solution.py:589
Async XLA Ops:
  8.9 11.5 %copy-start.2 = (bf16[112,98]{0,1:T(8,128)(2,1)S(1)}, bf16[112,98]{0,1:T(8,128)(2,1)}, u32[]{:S(2)}) copy-start(bf16[112,98]{0,1:T(8,128)(2,1)} %param.20) | copy-start | bytes 65860
  8.9 12.2 %copy-start.3 = (bf16[128,98]{0,1:T(8,128)(2,1)S(1)}, bf16[128,98]{0,1:T(8,128)(2,1)}, u32[]{:S(2)}) copy-start(bf16[128,98]{0,1:T(8,128)(2,1)} %param.18) | copy-start | bytes 75268
  8.9 49.6 %all-to-all-start = ((bf16[128,8,1408]{2,1,0:T(8,128)(2,1)}), bf16[128,8,1408]{2,1,0:T(8,128)(2,1)S(1)}, u32[]{:S(2)}, u32[]{:S(2)}) async-start(bf16[128,8,1408]{2,1,0:T(8,128)(2,1)} %bitcast.13), calls=%async_computation | async-start | bytes 5767168 | tf_op jit(solution)/shard_map/all_to_all | solution.py:558
  58.6 1.6 %copy-start = (bf16[128,8,1408]{2,1,0:T(8,128)(2,1)}, bf16[128,8,1408]{2,1,0:T(8,128)(2,1)S(1)}, u32[]{:S(2)}) copy-start(bf16[128,8,1408]{2,1,0:T(8,128)(2,1)S(1)} %all-to-all-done) | copy-start | bytes 8650756
  93.1 14.9 %all-to-all-start.1 = ((f32[128,2,128]{2,1,0:T(2,128)}), f32[128,2,128]{2,1,0:T(2,128)S(1)}, u32[]{:S(2)}, u32[]{:S(2)}) async-start(f32[128,2,128]{2,1,0:T(2,128)} %bitcast.15), calls=%async_computation.1 | async-start | bytes 262144 | tf_op jit(solution)/shard_map/all_to_all | solution.py:577
  108.0 0.7 copy-start.1

commit v3 on v2

--- a/solution.py
+++ b/solution.py
@@ -84,7 +84,7 @@
 
 def pack(me, map_row, dyn_state, devices):
     fields, levels, columns = dyn_state.shape
-    steps = fields // 8
+    steps = 1
     rows = devices * CAP * 2
     return pl.pallas_call(
         pack_kernel,
@@ -92,14 +92,14 @@
         in_specs=[
             pl.BlockSpec(memory_space=pltpu.SMEM),
             pl.BlockSpec((1, columns), lambda i: (0, 0)),
-            pl.BlockSpec((8, levels, columns), lambda i: (jnp.minimum(i, steps - 1), 0, 0)),
+            pl.BlockSpec((fields, levels, columns), lambda i: (jnp.minimum(i, steps - 1), 0, 0)),
         ],
         out_specs=[
-            pl.BlockSpec((rows, 256), lambda i: (0, i)),
+            pl.BlockSpec((rows, fields * 32), lambda i: (0, i)),
             pl.BlockSpec((devices * CAP, columns), lambda i: (0, 0)),
         ],
         out_shape=[
-            jax.ShapeDtypeStruct((rows, steps * 256 + 128), BF16),
+            jax.ShapeDtypeStruct((rows, fields * 32 + 128), BF16),
             jax.ShapeDtypeStruct((devices * CAP, columns), BF16),
         ],
         scratch_shapes=[
@@ -440,7 +440,7 @@
                 )
             return 0
 
-        lax.fori_loop(0, pairs // 2, two_pairs, 0, unroll=4)
+        lax.fori_loop(0, pairs // 2, two_pairs, 0, unroll=8)
         if tile < tiles:
             turn(tile)
 
@@ -584,6 +584,7 @@
         cost_estimate=pl.CostEstimate(
             flops=4 * levels * columns * columns, bytes_accessed=MIB, transcendentals=0
         ),
+        compiler_params=pltpu.CompilerParams(vmem_limit_bytes=8 * MIB),
         name="local",
     )(me, map_row, heat)
     heating = pl.pallas_call(
@@ -594,6 +595,7 @@
         cost_estimate=pl.CostEstimate(
             flops=8 * levels * columns * columns, bytes_accessed=MIB, transcendentals=0
         ),
+        compiler_params=pltpu.CompilerParams(vmem_limit_bytes=8 * MIB),
         name="unpack",
     )(local, pick, returned)
     return heating, surface

time: 111 us -> 108 us (0.973)
  Pallas kernels: 54 us -> 49.8 us
    pallas_call x1, Pallas kernels: 1.88 us -> 0.31 us  [shards(): pl.pallas_call(local_kernel, in_specs=[pl.BlockSpec(memory_space=pltpu.SM...]
    unnamed x10 -> x14, local copies, waits for them, and re-layouts: 3.7 us -> 3.95 us
  transfers between devices with their start and end apart: 2 -> 2, of which waited for: 2 -> 2; matrix products, arithmetic and copies ran while one was open for 1% -> 1% of each run, Pallas kernels for 10% -> 8%
where the time goes in v3:
time: 108 us
  Pallas kernels  49.8 us (46%)
  waiting for transfers between devices  36.8 us (34%)
  starting transfers between devices  16.3 us (15%)
  local copies, waits for them, and re-layouts  3.95 us (4%)
    pallas_call x1, Pallas kernels, flux(): pl.pallas_call(flux_kernel, in_specs=[pl.BlockSpec(memory_space=pl.ANY)]...  32.4 us
    all_to_all x1, waiting for transfers between devices, shards(): swap(outgoing.reshape(devices, 2 * CAP, width))  28 us
    all_to_all x1, starting transfers between devices, shards(): swap(outgoing.reshape(devices, 2 * CAP, width))  11.5 us
    all_to_all x1, waiting for transfers between devices, shards(): returned = swap(back.reshape(devices, 2, 128)).reshape(devices * 2, 128)  8.82 us
    pallas_call x1, Pallas kernels, base(): pl.pallas_call(base_kernel, grid=(levels // depth,), in_specs=[pl.BlockSp...  8.67 us
    pallas_call x1, Pallas kernels, pack(): pl.pallas_call(pack_kernel, grid=(steps + 1,), in_specs=[pl.BlockSpec(mem...  7.29 us
    all_to_all x1, starting transfers between devices, shards(): returned = swap(back.reshape(devices, 2, 128)).reshape(devices * 2, 128)  4.8 us
    unnamed x14, local copies, waits for them, and re-layouts  3.95 us
  transfers between devices with their start and end apart: 2, of which 2 were waited for; matrix products, arithmetic and copies ran while one was open for 1% of the time, Pallas kernels for 8%

profile of v3, /device:TPU:1, one launch (start us, length us, event | category | flops | bytes accessed | tf_op | source)
XLA Modules:
  0.0 107.5 jit_solution(3057946376319809647)
XLA Ops:
  0.6 7.3 %pack.1 = (bf16[1024,1408]{1,0:T(8,128)(2,1)}, bf16[512,512]{1,0:T(8,128)(2,1)}) custom-call(s32[1]{0:T(128)} %bitcast.me_ref, s32[1,512]{1,0:T(1,128)} %bitcast.13, bf16[40,64,512]{2,1,0:T(8,128)(2,1)} %dyn_ref.3), custom_call_target="tpu_custom_call" | custom-call | flops 2684354560 | bytes 6291456 | tf_op jit(solution)/shard_map/pack/pallas_call | solution.py:89
  7.9 0.0 copy-start.4
  7.9 0.0 copy-start.5
  7.9 11.5 %all-to-all-start = ((bf16[128,8,1408]{2,1,0:T(8,128)(2,1)}), bf16[128,8,1408]{2,1,0:T(8,128)(2,1)S(1)}, u32[]{:S(2)}, u32[]{:S(2)}) async-start(bf16[128,8,1408]{2,1,0:T(8,128)(2,1)} %bitcast.17), calls=%async_computation | async-start | bytes 5767168 | tf_op jit(solution)/shard_map/all_to_all | solution.py:558
  19.4 0.0 copy-done.4
  19.5 0.7 copy.14.short_ref
  20.2 0.0 copy-done.5
  20.2 0.7 copy.13.long_ref
  20.9 8.7 %base.1 = (bf16[4,64,64,128]{3,2,1,0:T(8,128)(2,1)}, bf16[2,40,32,512]{3,2,1,0:T(8,128)(2,1)}, bf16[240,224]{1,0:T(8,128)(2,1)}, f32[240,128]{1,0:T(8,128)}) custom-call(s32[1]{0:T(128)} %bitcast.me_ref, s32[1,512]{1,0:T(1,128)} %bitcast.14, bf16[40,64,512]{2,1,0:T(8,128)(2,1)} %dyn_ref.3, bf16[58,64,512]{2,1,0:T(8,128)(2,1)} %aer_ref.1, ...), custom_call_target="tpu_custom_call" | custom-call | flops 1342177280 | bytes 14680064 | tf_op jit(solution)/shard_map/base/pallas_call | solution.py:184
  29.6 28.0 %all-to-all-done = bf16[128,8,1408]{2,1,0:T(8,128)(2,1)S(1)} async-done(((bf16[128,8,1408]{2,1,0:T(8,128)(2,1)}), bf16[128,8,1408]{2,1,0:T(8,128)(2,1)S(1)}, u32[]{:S(2)}, u32[]{:S(2)}) %all-to-all-start) | async-done | bytes 2883616 | tf_op jit(solution)/shard_map/all_to_all | solution.py:558
  57.6 0.0 copy-start.3
  57.6 1.6 %copy-done.3 = bf16[128,8,1408]{2,1,0:T(8,128)(2,1)} copy-done((bf16[128,8,1408]{2,1,0:T(8,128)(2,1)}, bf16[128,8,1408]{2,1,0:T(8,128)(2,1)S(1)}, u32[]{:S(2)}) %copy-start.3) | copy-done | bytes 2883608
  59.2 0.0 copy-start.2
  59.2 0.0 copy-start
  59.2 32.4 %flux.1 = (f32[64,512]{1,0:T(8,128)}, f32[2,512]{1,0:T(2,128)}, f32[256,128]{1,0:T(8,128)}) custom-call(bf16[1024,1408]{1,0:T(8,128)(2,1)} %bitcast.16, bf16[4,64,64,128]{3,2,1,0:T(8,128)(2,1)} %get-tuple-element.12.aero_hbm, bf16[2,40,32,512]{3,2,1,0:T(8,128)(2,1)} %get-tuple-element.13.kept_hbm, bf16[240,224]{1,0:T(8,128)(2,1)} %get-tuple-element.14.k_ref, ...), custom_call_target="tpu_custom_call" | custom-call | flops 1966080000 | bytes 12582912 | tf_op jit(solution)/shard_map/flux/pallas_call | solution.py:476
  91.6 4.8 %all-to-all-start.1 = ((f32[128,2,128]{2,1,0:T(2,128)}), f32[128,2,128]{2,1,0:T(2,128)S(1)}, u32[]{:S(2)}, u32[]{:S(2)}) async-start(f32[128,2,128]{2,1,0:T(2,128)} %bitcast.18), calls=%async_computation.1 | async-start | bytes 262144 | tf_op jit(solution)/shard_map/all_to_all | solution.py:577
  96.4 0.0 copy-done.2
  96.4 0.0 copy-start.1
  96.4 0.9 copy-done.1
  97.3 0.3 local.1.local_ref
  97.6 8.8 %all-to-all-done.1 = f32[128,2,128]{2,1,0:T(2,128)S(1)} async-done(((f32[128,2,128]{2,1,0:T(2,128)}), f32[128,2,128]{2,1,0:T(2,128)S(1)}, u32[]{:S(2)}, u32[]{:S(2)}) %all-to-all-start.1) | async-done | bytes 131104 | tf_op jit(solution)/shard_map/all_to_all | solution.py:577
  106.4 0.0 copy-done
  106.4 1.1 %unpack.1 = f32[64,512]{1,0:T(8,128)} custom-call(f32[64,512]{1,0:T(8,128)S(1)} %local.1.local_ref, bf16[512,512]{1,0:T(8,128)(2,1)S(1)} %copy-done, f32[256,128]{1,0:T(8,128)S(1)} %bitcast.12), custom_call_target="tpu_custom_call" | custom-call | flops 134217728 | bytes 1048576 | tf_op jit(solution)/shard_map/unpack/pallas_call | solution.py:590
Async XLA Ops:
  7.9 11.5 %copy-start.4 = (bf16[112,98]{0,1:T(8,128)(2,1)S(1)}, bf16[112,98]{0,1:T(8,128)(2,1)}, u32[]{:S(2)}) copy-start(bf16[112,98]{0,1:T(8,128)(2,1)} %param.20) | copy-start | bytes 65860
  7.9 12.2 %copy-start.5 = (bf16[128,98]{0,1:T(8,128)(2,1)S(1)}, bf16[128,98]{0,1:T(8,128)(2,1)}, u32[]{:S(2)}) copy-start(bf16[128,98]{0,1:T(8,128)(2,1)} %param.18) | copy-start | bytes 75268
  7.9 49.6 %all-to-all-start = ((bf16[128,8,1408]{2,1,0:T(8,128)(2,1)}), bf16[128,8,1408]{2,1,0:T(8,128)(2,1)S(1)}, u32[]{:S(2)}, u32[]{:S(2)}) async-start(bf16[128,8,1408]{2,1,0:T(8,128)(2,1)} %bitcast.17), calls=%async_computation | async-start | bytes 5767168 | tf_op jit(solution)/shard_map/all_to_all | solution.py:558
  57.6 1.6 %copy-start.3 = (bf16[128,8,1408]{2,1,0:T(8,128)(2,1)}, bf16[128,8,1408]{2,1,0:T(8,128)(2,1)S(1)}, u32[]{:S(2)}) copy-start(bf16[128,8,1408]{2,1,0:T(8,128)(2,1)S(1)} %all-to-all-done) | copy-start | bytes 8650756
  59.2 37.2 %copy-start.2 = (s32[512]{0:T(512)S(1)}, s32[512]{0:T(512)}, u32[]{:S(2)}) copy-start(s32[512]{0:T(512)} %param.12) | copy-start | bytes 6148
  59.2 47.2 %copy-start = (bf16[512,512]{1,0:T(8,128)(2,1)S(1)}, bf16[512,512]{1,0:T(8,128)(2,1)}, u32[]{:S(2)}) copy-start(bf16[512,512]{1,0:T(8,128)(2,1)} %get-tuple-element.17.pick_ref) | copy-start | bytes 1572868
  91.6 14.9 %all-to-all-start.1 = ((f32[128,2,128]{2,1,0:T(2,128)}), f32[128,2,128]{2,1,0:T(2,128)S(1)}, u32[]{:S(2)}, u32[]{:S(2)}) async-start(f32[128,2,128]{2,1,0:T(2,128)} %bitcast.18), calls=%async_computation.1 | async-start | bytes 262144 | tf_op jit(solution)/shard_map/all_to_all | solution.py:577
  96.4 0.9 copy-start.1

commit v4 on v3

--- a/solution.py
+++ b/solution.py
@@ -211,7 +211,7 @@
             pltpu.VMEM((tiles, extra * depth, 128), F32),
             pltpu.VMEM((glw + gsw, 2 * (HEAD + TAIL)), F32),
         ],
-        compiler_params=pltpu.CompilerParams(vmem_limit_bytes=56 * MIB),
+        compiler_params=pltpu.CompilerParams(vmem_limit_bytes=62 * MIB),
         cost_estimate=pl.CostEstimate(
             flops=2 * fields * levels * columns * columns, bytes_accessed=14 * MIB, transcendentals=0
         ),

time: 108 us -> 106 us (0.981)
  local copies, waits for them, and re-layouts: 3.95 us -> 2.36 us
    unnamed x14 -> x12, local copies, waits for them, and re-layouts: 3.95 us -> 2.36 us
where the time goes in v4:
time: 106 us
  Pallas kernels  49.7 us (47%)
  waiting for transfers between devices  36.5 us (34%)
  starting transfers between devices  16.7 us (16%)
  local copies, waits for them, and re-layouts  2.36 us (2%)
    pallas_call x1, Pallas kernels, flux(): pl.pallas_call(flux_kernel, in_specs=[pl.BlockSpec(memory_space=pl.ANY)]...  32.4 us
    all_to_all x1, waiting for transfers between devices, shards(): swap(outgoing.reshape(devices, 2 * CAP, width))  27.7 us
    all_to_all x1, starting transfers between devices, shards(): swap(outgoing.reshape(devices, 2 * CAP, width))  11.9 us
    all_to_all x1, waiting for transfers between devices, shards(): returned = swap(back.reshape(devices, 2, 128)).reshape(devices * 2, 128)  8.82 us
    pallas_call x1, Pallas kernels, base(): pl.pallas_call(base_kernel, grid=(levels // depth,), in_specs=[pl.BlockSp...  8.67 us
    pallas_call x1, Pallas kernels, pack(): pl.pallas_call(pack_kernel, grid=(steps + 1,), in_specs=[pl.BlockSpec(mem...  7.26 us
    all_to_all x1, starting transfers between devices, shards(): returned = swap(back.reshape(devices, 2, 128)).reshape(devices * 2, 128)  4.81 us
    unnamed x12, local copies, waits for them, and re-layouts  2.36 us
  transfers between devices with their start and end apart: 2, of which 2 were waited for; matrix products, arithmetic and copies ran while one was open for 1% of the time, Pallas kernels for 8%

profile of v4, /device:TPU:1, one launch (start us, length us, event | category | flops | bytes accessed | tf_op | source)
XLA Modules:
  0.0 106.0 jit_solution(10926936270244081955)
XLA Ops:
  0.6 7.3 %pack.1 = (bf16[1024,1408]{1,0:T(8,128)(2,1)}, bf16[512,512]{1,0:T(8,128)(2,1)}) custom-call(s32[1]{0:T(128)} %bitcast.me_ref, s32[1,512]{1,0:T(1,128)} %bitcast.13, bf16[40,64,512]{2,1,0:T(8,128)(2,1)} %dyn_ref.3), custom_call_target="tpu_custom_call" | custom-call | flops 2684354560 | bytes 6291456 | tf_op jit(solution)/shard_map/pack/pallas_call | solution.py:89
  7.9 0.0 copy-start.3
  7.9 0.0 copy-start.4
  7.9 11.9 %all-to-all-start = ((bf16[128,8,1408]{2,1,0:T(8,128)(2,1)}), bf16[128,8,1408]{2,1,0:T(8,128)(2,1)}, u32[]{:S(2)}, u32[]{:S(2)}) async-start(bf16[128,8,1408]{2,1,0:T(8,128)(2,1)} %bitcast.16), calls=%async_computation | async-start | bytes 5767168 | tf_op jit(solution)/shard_map/all_to_all | solution.py:558
  19.8 0.0 copy-done.3
  19.8 0.7 copy.14.short_ref
  20.6 0.0 copy-done.4
  20.6 0.7 copy.13.long_ref
  21.3 8.7 %base.1 = (bf16[4,64,64,128]{3,2,1,0:T(8,128)(2,1)}, bf16[2,40,32,512]{3,2,1,0:T(8,128)(2,1)}, bf16[240,224]{1,0:T(8,128)(2,1)}, f32[240,128]{1,0:T(8,128)}) custom-call(s32[1]{0:T(128)} %bitcast.me_ref, s32[1,512]{1,0:T(1,128)} %bitcast.14, bf16[40,64,512]{2,1,0:T(8,128)(2,1)} %dyn_ref.3, bf16[58,64,512]{2,1,0:T(8,128)(2,1)} %aer_ref.1, ...), custom_call_target="tpu_custom_call" | custom-call | flops 1342177280 | bytes 14680064 | tf_op jit(solution)/shard_map/base/pallas_call | solution.py:184
  30.0 27.7 %all-to-all-done = bf16[128,8,1408]{2,1,0:T(8,128)(2,1)} async-done(((bf16[128,8,1408]{2,1,0:T(8,128)(2,1)}), bf16[128,8,1408]{2,1,0:T(8,128)(2,1)}, u32[]{:S(2)}, u32[]{:S(2)}) %all-to-all-start) | async-done | bytes 2883616 | tf_op jit(solution)/shard_map/all_to_all | solution.py:558
  57.6 0.0 copy-start.2
  57.7 0.0 copy-start
  57.7 32.4 %flux.1 = (f32[64,512]{1,0:T(8,128)}, f32[2,512]{1,0:T(2,128)}, f32[256,128]{1,0:T(8,128)}) custom-call(bf16[1024,1408]{1,0:T(8,128)(2,1)} %bitcast.3.recv_hbm, bf16[4,64,64,128]{3,2,1,0:T(8,128)(2,1)} %get-tuple-element.12.aero_hbm, bf16[2,40,32,512]{3,2,1,0:T(8,128)(2,1)} %get-tuple-element.13.kept_hbm, bf16[240,224]{1,0:T(8,128)(2,1)} %get-tuple-element.14.k_ref, ...), custom_call_target="tpu_custom_call" | custom-call | flops 1966080000 | bytes 12582912 | tf_op jit(solution)/shard_map/flux/pallas_call | solution.py:476
  90.0 4.8 %all-to-all-start.1 = ((f32[128,2,128]{2,1,0:T(2,128)}), f32[128,2,128]{2,1,0:T(2,128)S(1)}, u32[]{:S(2)}, u32[]{:S(2)}) async-start(f32[128,2,128]{2,1,0:T(2,128)} %bitcast.17), calls=%async_computation.1 | async-start | bytes 262144 | tf_op jit(solution)/shard_map/all_to_all | solution.py:577
  94.8 0.0 copy-done.2
  94.9 0.0 copy-start.1
  94.9 0.9 copy-done.1
  95.8 0.3 local.1.local_ref
  96.1 8.8 %all-to-all-done.1 = f32[128,2,128]{2,1,0:T(2,128)S(1)} async-done(((f32[128,2,128]{2,1,0:T(2,128)}), f32[128,2,128]{2,1,0:T(2,128)S(1)}, u32[]{:S(2)}, u32[]{:S(2)}) %all-to-all-start.1) | async-done | bytes 131104 | tf_op jit(solution)/shard_map/all_to_all | solution.py:577
  104.9 0.0 copy-done
  104.9 1.1 %unpack.1 = f32[64,512]{1,0:T(8,128)} custom-call(f32[64,512]{1,0:T(8,128)S(1)} %local.1.local_ref, bf16[512,512]{1,0:T(8,128)(2,1)S(1)} %copy-done, f32[256,128]{1,0:T(8,128)S(1)} %bitcast.12), custom_call_target="tpu_custom_call" | custom-call | flops 134217728 | bytes 1048576 | tf_op jit(solution)/shard_map/unpack/pallas_call | solution.py:590
Async XLA Ops:
  7.9 11.9 %copy-start.3 = (bf16[112,98]{0,1:T(8,128)(2,1)S(1)}, bf16[112,98]{0,1:T(8,128)(2,1)}, u32[]{:S(2)}) copy-start(bf16[112,98]{0,1:T(8,128)(2,1)} %param.20) | copy-start | bytes 65860
  7.9 12.7 %copy-start.4 = (bf16[128,98]{0,1:T(8,128)(2,1)S(1)}, bf16[128,98]{0,1:T(8,128)(2,1)}, u32[]{:S(2)}) copy-start(bf16[128,98]{0,1:T(8,128)(2,1)} %param.18) | copy-start | bytes 75268
  7.9 49.8 %all-to-all-start = ((bf16[128,8,1408]{2,1,0:T(8,128)(2,1)}), bf16[128,8,1408]{2,1,0:T(8,128)(2,1)}, u32[]{:S(2)}, u32[]{:S(2)}) async-start(bf16[128,8,1408]{2,1,0:T(8,128)(2,1)} %bitcast.16), calls=%async_computation | async-start | bytes 5767168 | tf_op jit(solution)/shard_map/all_to_all | solution.py:558
  57.6 37.2 %copy-start.2 = (s32[512]{0:T(512)S(1)}, s32[512]{0:T(512)}, u32[]{:S(2)}) copy-start(s32[512]{0:T(512)} %param.12) | copy-start | bytes 6148
  57.7 47.2 %copy-start = (bf16[512,512]{1,0:T(8,128)(2,1)S(1)}, bf16[512,512]{1,0:T(8,128)(2,1)}, u32[]{:S(2)}) copy-start(bf16[512,512]{1,0:T(8,128)(2,1)} %get-tuple-element.17.pick_ref) | copy-start | bytes 1572868
  90.0 14.9 %all-to-all-start.1 = ((f32[128,2,128]{2,1,0:T(2,128)}), f32[128,2,128]{2,1,0:T(2,128)S(1)}, u32[]{:S(2)}, u32[]{:S(2)}) async-start(f32[128,2,128]{2,1,0:T(2,128)} %bitcast.17), calls=%async_computation.1 | async-start | bytes 262144 | tf_op jit(solution)/shard_map/all_to_all | solution.py:577
  94.9 0.9 copy-start.1
